TPU v7x, 512 devices: a whole 4x4x16 slice. The times are simulated.
512 devices in a mesh: samples: 64 (over z, y), variants: 8 (over x, core).
Axes of the slice: x: 4, y: 4, z: 16, core: 2. Of those that a mesh axis runs over, the one named last changes fastest.
Arguments:
- genotypes: bfloat16 [49152, 16384], P('samples', 'variants'), may hold values from -6 to 6
- basis_in: bfloat16 [49152, 256], P('samples'), may hold values from -0.02734375 to 0.02734375
Outputs:
- basis_out: float32 [49152, 256], P('samples')
- factor: float32 [256, 256], replicated
All inputs are finite; a program needn't handle non-finite values.
Results may differ from a plain program's by a relative error of at most 0.0026.
Values may be sent and summed in bfloat16 or wider, within the bound.
A program may use at most 64 MiB of HBM per device.

v0:
```python
import jax
import jax.numpy as jnp
from jax import lax
from jax.sharding import PartitionSpec as P


def local(genotypes, basis_in):
    samp_rows, var_cols = genotypes.shape
    n_samples = lax.axis_size("samples")
    n_variants = lax.axis_size("variants")
    total_samples = samp_rows * n_samples
    scale = 1.0 / (var_cols * n_variants) ** 0.5
    contract = (((0,), (0,)), ((), ()))
    term = lax.dot_general(genotypes, basis_in, contract, preferred_element_type=jnp.float32)
    loadings = lax.psum(term, "samples").astype(jnp.bfloat16)
    partial_scores = jnp.dot(genotypes, loadings, preferred_element_type=jnp.float32) * scale
    scores = lax.psum(partial_scores, "variants")
    gram = jnp.dot(scores.T, scores, precision=lax.Precision.HIGHEST) / total_samples
    lower = jnp.linalg.cholesky(lax.psum(gram, "samples"))
    new_rows = lax.linalg.triangular_solve(lower, scores.T, left_side=True, lower=True).T
    return (new_rows, lower.T)


def solution(mesh):
    placed = (P("samples", "variants"), P("samples", None))
    return jax.shard_map(
        local, mesh=mesh, in_specs=placed, out_specs=(P("samples", None), P()), check_vma=False
    )
```

profile of v0, /device:TPU:1, one launch (start us, length us, event | category | flops | bytes accessed | tf_op | source)
XLA Modules:
  0.0 733.0 jit_solution(365627651752314517)
XLA Ops:
  7.2 0.0 copy-start
  7.2 0.0 all-reduce.5.cloned.1.call-start
  7.2 1.8 copy-done
  9.1 3.4 fusion.13
  12.4 255.5 %all-reduce.8 = bf16[2048,256]{1,0:T(8,128)(2,1)} all-reduce(f32[2048,256]{1,0:T(8,128)} %fusion.13), channel_id=1, replica_groups=mesh['samples'=64,'variants'=8] {'samples'}, use_global_device_ids=true, to_apply=%region_0.0 | all-reduce | flops 524288 | bytes 3145728 | tf_op jit(solution)/shard_map/psum | solution.py:15
  268.0 3.1 fusion
  271.1 0.0 all-reduce.5.cloned.1.call-update
  271.1 0.2 all-reduce.7.cloned.1.call-start
  271.3 122.3 %all-reduce.5.cloned.1.call-done = f32[768,256]{0,1:T(8,128)} async-done(((f32[768,256]{0,1:T(8,128)}), f32[768,256]{0,1:T(8,128)}) %all-reduce.5.cloned.1.call-update) | async-done | bytes 786448 | tf_op jit(solution)/shard_map/psum | solution.py:17
  393.7 2.9 convolution_multiply_fusion.1
  396.6 0.0 all-reduce.7.cloned.1.call-update
  396.6 254.4 %all-reduce.7.cloned.1.call-done = f32[256,256]{0,1:T(8,128)} async-done(((f32[256,256]{0,1:T(8,128)}), f32[256,256]{0,1:T(8,128)}) %all-reduce.7.cloned.1.call-update) | async-done | bytes 262160 | tf_op jit(solution)/shard_map/psum | solution.py:19
  651.0 1.1 copy.5
  652.1 1.0 fusion.4
  653.1 0.0 copy-start.3
  653.1 0.7 copy-done.3
  653.8 11.7 %cholesky.50 = f32[128,128]{1,0:T(8,128)S(1)} custom-call(f32[128,128]{1,0:T(8,128)S(1)} %cholesky.118), custom_call_target="Cholesky" | custom-call | tf_op jit(solution)/shard_map/jit(cholesky)/cholesky | solution.py:19
  665.6 9.8 %custom-call.14 = f32[1,128,128]{1,2,0:T(8,128)S(1)} custom-call(f32[1,128,128]{2,1,0:T(8,128)S(1)} %get-tuple-element.27), custom_call_target="InvertDiagBlocksLowerTriangular" | custom-call | tf_op jit(solution)/shard_map/jit(cholesky)/cholesky | solution.py:19
  675.4 1.0 constant_dynamic-update-slice_fusion.1
  676.5 1.1 convolution_subtract_fusion.1
  677.6 11.7 %cholesky.105 = f32[128,128]{1,0:T(8,128)S(1)} custom-call(f32[128,128]{1,0:T(8,128)S(1)} %convolution_subtract_fusion.1), custom_call_target="Cholesky" | custom-call | tf_op jit(solution)/shard_map/jit(cholesky)/cholesky | solution.py:19
  689.3 0.0 copy-start.1
  689.3 0.7 compare_reduce_fusion
  691.2 0.0 copy-done.1
  691.2 1.7 fusion.6
  692.9 0.1 triangular_solve.57
  693.0 5.1 while.1
  693.0 0.6 fusion.25
  693.7 1.9 bitcast_dynamic-update-slice_fusion.2
  695.6 0.6 fusion.25
  696.2 1.9 bitcast_dynamic-update-slice_fusion.2
  698.1 20.5 %custom-call.15 = f32[2,128,128]{1,2,0:T(8,128)S(1)} custom-call(f32[2,128,128]{2,1,0:T(8,128)} %get-tuple-element.9), custom_call_target="InvertDiagBlocksLowerTriangular" | custom-call | tf_op jit(solution)/shard_map/triangular_solve | solution.py:20
  718.6 1.5 fusion.2
  720.1 1.5 convolution_subtract_fusion
  721.6 0.0 copy-start.2
  721.6 0.5 fusion.8
  722.1 0.9 maximum_bitcast_fusion
  723.1 2.3 copy.6
  725.3 0.0 copy-done.2
  725.3 0.8 copy.7
  (8 shorter events, 0.1 us)
Async XLA Ops:
  7.2 1.9 copy-start
  7.2 386.5 %all-reduce.5.cloned.1.call-start = ((), (), s32[]{:S(2)}) async-start(), calls=%async_computation | async-start | bytes 1572864 | tf_op jit(solution)/shard_map/psum | solution.py:17
  271.1 379.9 %all-reduce.7.cloned.1.call-start = ((), (), s32[]{:S(2)}) async-start(), calls=%async_computation.1 | async-start | bytes 524288 | tf_op jit(solution)/shard_map/psum | solution.py:19
  653.1 0.7 copy-start.3
  689.3 1.9 copy-start.1
  721.6 3.7 copy-start.2
Sparse Core Ops, SparseCore 0:
  271.2 122.3 all-reduce.4
  398.0 252.9 all-reduce.6
where the time goes:
time: 743 us; the launch traced here: 733 us
  waiting for transfers between devices  377 us (51%)
  blocking collectives  256 us (34%)
  other arithmetic  58.1 us (8%)
  between operations  15.3 us (2%)
  matrix products  15 us (2%)
  local copies, waits for them, and re-layouts  11.9 us (2%)
    psum x1, blocking collectives, local(): loadings = lax.psum(term, 'samples').astype(jnp.bfloat16)  256 us
    psum x1, waiting for transfers between devices, local(): lower = jnp.linalg.cholesky(lax.psum(gram, 'samples'))  254 us
    psum x1, waiting for transfers between devices, local(): scores = lax.psum(partial_scores, 'variants')  122 us
    another operation x6, other arithmetic, local(): lower = jnp.linalg.cholesky(lax.psum(gram, 'samples'))  34 us
    another operation x2, other arithmetic, local(): lax.linalg.triangular_solve(lower, scores.T, left_side=True, lower=True)  20.5 us
  transfers between devices with their start and end apart: 2, of which 2 were waited for; matrix products, arithmetic and copies ran while one was open for 0% of the time, Pallas kernels for 0%

commit v1 on v0

v1 whole, which is shorter than its diff:
```python
import functools

import jax
import jax.numpy as jnp
from jax import lax
from jax.experimental import pallas as pl
from jax.experimental.pallas import tpu as pltpu
from jax.sharding import PartitionSpec as P

MESH = pl.DeviceIdType.MESH
NZ, NY, NX, NC = 16, 4, 4, 2
NQ = 4
F32, BF16 = jnp.float32, jnp.bfloat16
SHIFT = 4096.0
LOG_SHIFT = 8.317766166719343


def encode(x):
    s = x * SHIFT
    s2 = s * s
    return (s2 * s2 * s).astype(BF16)


def decode(y):
    y = y.astype(F32)
    r = jnp.exp(jnp.log(jnp.abs(y)) * 0.2 - LOG_SHIFT)
    return jnp.where(y < 0, -r, r)


def dot(a, b, dims, **kw):
    return lax.dot_general(a, b, (dims, ((), ())), preferred_element_type=F32, **kw)


def comm_kernel(
    scale, total, g_hbm, b_ref, scores_ref, gram_ref,
    gbuf, tf, ysend, yrecv, sf, zsend, zrecv, lall,
    spart, crecv, xrecv, sall, gp, gcrecv, gxrecv, gx, gyrecv, gzall, gall,
    load_sem, ys, yr, zs, zr, ls, lr, us, ur, ps, pr,
):
    samp, var = lax.axis_index("samples"), lax.axis_index("variants")
    z, y = lax.div(samp, NY), lax.rem(samp, NY)
    x, c = lax.div(var, NC), lax.rem(var, NC)

    def dev(dz, dy, dx, dc):
        return (
            lax.rem(z + dz, NZ) * NY + lax.rem(y + dy, NY),
            lax.rem(x + dx, NX) * NC + lax.rem(c + dc, NC),
        )

    def start(src, dst, send, recv, to):
        pltpu.make_async_remote_copy(
            src_ref=src, dst_ref=dst, send_sem=send, recv_sem=recv,
            device_id=to, device_id_type=MESH,
        ).start()

    def wait(ref, sem):
        pltpu.make_async_copy(ref, ref, sem).wait()

    def rows(i, n):
        return pl.ds(pl.multiple_of(i * n, n), n)

    plane = [(dy, dx, dc) for dy in range(NY) for dx in range(NX) for dc in range(NC)][1:]
    partners = [(dz, 0, 0, 0) for dz in range(1, NZ)] + [(0,) + p for p in plane]

    cols = gbuf.shape[2]
    loads = [
        pltpu.make_async_copy(g_hbm.at[:, pl.ds(q * cols, cols)], gbuf.at[q], load_sem.at[q])
        for q in range(NQ)
    ]
    for load in loads:
        load.start()
    barrier = pltpu.get_barrier_semaphore()
    for p in partners:
        pl.semaphore_signal(barrier, inc=1, device_id=dev(*p), device_id_type=MESH)

    def term(q):
        loads[q].wait()
        t = dot(b_ref[...], gbuf[q], ((0,), (0,)))
        for i in range(NY):
            tf[q, i] = t[:, i * 128:(i + 1) * 128]

    def send_y(q):
        for dy in range(1, NY):
            to = lax.rem(y + dy, NY)
            ysend[q, dy - 1] = encode(tf[q, to])
            start(ysend.at[q, dy - 1], yrecv.at[q, dy - 1], ys.at[q], yr.at[q], dev(0, dy, 0, 0))

    term(0)
    pl.semaphore_wait(barrier, len(partners))
    send_y(0)
    for q in range(1, NQ):
        term(q)
        send_y(q)
    for q in range(NQ):
        wait(yrecv.at[q], yr.at[q])
        s = tf[q, y]
        for i in range(NY - 1):
            s = s + decode(yrecv[q, i])
        sf[q] = s
        zsend[q] = encode(s)
        for dz in range(1, NZ):
            to = lax.rem(z + dz, NZ)
            start(zsend.at[q, rows(to, 16)], zrecv.at[q, pl.ds((dz - 1) * 16, 16)], zs.at[q], zr.at[q], dev(dz, 0, 0, 0))
    for q in range(NQ):
        wait(zrecv.at[q], zr.at[q])
        s = sf[q, rows(z, 16)]
        for i in range(NZ - 1):
            s = s + decode(zrecv[q, i * 16:(i + 1) * 16])
        lall[q, y, rows(z, 16)] = s.astype(BF16)
        for dz in range(1, NZ):
            mine = lall.at[q, y, rows(z, 16)]
            start(mine, mine, ls.at[q], lr.at[q], dev(dz, 0, 0, 0))
    for q in range(NQ):
        wait(lall.at[q, y, pl.ds(0, 240)], lr.at[q])
        for dy in range(1, NY):
            mine = lall.at[q, y]
            start(mine, mine, us.at[q], ur.at[q], dev(0, dy, 0, 0))
    for q in range(NQ):
        wait(lall.at[q, pl.ds(0, 3)], ur.at[q])
        part = jnp.concatenate([lall[q, i] for i in range(NY)], axis=1)
        t = dot(gbuf[q], part, ((1,), (1,)))
        if q == 0:
            spart[...] = t
        else:
            spart[...] += t
    half, chunk = spart.shape[0] // NC, spart.shape[0] // (NC * NX)
    other = lax.rem(c + 1, NC)
    start(spart.at[rows(other, half)], crecv, ps.at[0], pr.at[0], dev(0, 0, 0, 1))
    wait(crecv, pr.at[0])
    crecv[...] = crecv[...] + spart[rows(c, half)]
    for dx in range(1, NX):
        to = lax.rem(x + dx, NX)
        start(crecv.at[rows(to, chunk)], xrecv.at[dx - 1], ps.at[1], pr.at[1], dev(0, 0, dx, 0))
    wait(xrecv, pr.at[1])
    r = (((crecv[rows(x, chunk)] + xrecv[0]) + xrecv[1]) + xrecv[2]) * scale
    mine = c * NX + x
    sall[rows(mine, chunk)] = r
    gp[...] = dot(r, r, ((0,), (0,)), precision=lax.Precision.HIGHEST) * (1.0 / total)
    start(gp.at[rows(other, 128)], gcrecv, ps.at[2], pr.at[2], dev(0, 0, 0, 1))
    wait(gcrecv, pr.at[2])
    gcrecv[...] = gcrecv[...] + gp[rows(c, 128)]
    for dx in range(1, NX):
        to = lax.rem(x + dx, NX)
        start(gcrecv.at[rows(to, 32)], gxrecv.at[dx - 1], ps.at[3], pr.at[3], dev(0, 0, dx, 0))
    for dx in range(1, NX):
        own = sall.at[rows(mine, chunk)]
        start(own, own, ps.at[4], pr.at[4], dev(0, 0, dx, 0))
    wait(gxrecv, pr.at[3])
    gx[...] = ((gcrecv[rows(x, 32)] + gxrecv[0]) + gxrecv[1]) + gxrecv[2]
    for dy in range(1, NY):
        to = lax.rem(y + dy, NY)
        start(gx.at[rows(to, 8)], gyrecv.at[dy - 1], ps.at[5], pr.at[5], dev(0, dy, 0, 0))
    wait(gyrecv, pr.at[5])
    gzall[z] = ((gx[rows(y, 8)] + gyrecv[0]) + gyrecv[1]) + gyrecv[2]
    for dz in range(1, NZ):
        start(gzall.at[z], gzall.at[z], ps.at[6], pr.at[6], dev(dz, 0, 0, 0))
    wait(sall.at[pl.ds(0, 3 * chunk)], pr.at[4])
    own = sall.at[rows(c, half)]
    start(own, own, ps.at[7], pr.at[7], dev(0, 0, 0, 1))
    wait(gzall.at[pl.ds(0, NZ - 1)], pr.at[6])
    s = gzall[0]
    for i in range(1, NZ):
        s = s + gzall[i]
    own = gall.at[rows((c * NX + x) * NY + y, 8)]
    own[...] = s
    for p in plane:
        start(own, own, ps.at[8], pr.at[8], dev(0, *p))
    wait(sall.at[pl.ds(0, half)], pr.at[7])
    scores_ref[...] = sall[...]
    wait(gall.at[pl.ds(0, 248)], pr.at[8])
    gram_ref[...] = gall[...]
    for q in range(NQ):
        wait(ysend.at[q], ys.at[q])
        wait(zrecv.at[q], zs.at[q])
        wait(zrecv.at[q], ls.at[q])
        wait(lall.at[q, pl.ds(0, 3)], us.at[q])
    wait(crecv, ps.at[0])
    wait(xrecv, ps.at[1])
    wait(gcrecv, ps.at[2])
    wait(gxrecv, ps.at[3])
    wait(sall.at[pl.ds(0, 3 * chunk)], ps.at[4])
    wait(gyrecv, ps.at[5])
    wait(gzall.at[pl.ds(0, NZ - 1)], ps.at[6])
    wait(sall.at[pl.ds(0, half)], ps.at[7])
    wait(gall.at[pl.ds(0, 248)], ps.at[8])


def scores_and_gram(genotypes, basis_in):
    n, v = genotypes.shape
    k = basis_in.shape[1]
    total_samples = n * lax.axis_size("samples")
    scale = 1.0 / (v * lax.axis_size("variants")) ** 0.5
    part = v // NQ
    chunk = n // (NC * NX)
    dma = pltpu.SemaphoreType.DMA
    vmem = pl.BlockSpec(memory_space=pltpu.VMEM)
    return pl.pallas_call(
        functools.partial(comm_kernel, scale, total_samples),
        out_shape=[jax.ShapeDtypeStruct((n, k), F32), jax.ShapeDtypeStruct((k, k), F32)],
        in_specs=[pl.BlockSpec(memory_space=pl.ANY), vmem],
        out_specs=[vmem, vmem],
        scratch_shapes=[
            pltpu.VMEM((NQ, n, part), BF16),
            pltpu.VMEM((NQ, NY, k, 128), F32),
            pltpu.VMEM((NQ, NY - 1, k, 128), BF16),
            pltpu.VMEM((NQ, NY - 1, k, 128), BF16),
            pltpu.VMEM((NQ, k, 128), F32),
            pltpu.VMEM((NQ, k, 128), BF16),
            pltpu.VMEM((NQ, (NZ - 1) * 16, 128), BF16),
            pltpu.VMEM((NQ, NY, k, 128), BF16),
            pltpu.VMEM((n, k), F32),
            pltpu.VMEM((n // NC, k), F32),
            pltpu.VMEM((NX - 1, chunk, k), F32),
            pltpu.VMEM((n, k), F32),
            pltpu.VMEM((k, k), F32),
            pltpu.VMEM((k // NC, k), F32),
            pltpu.VMEM((NX - 1, 32, k), F32),
            pltpu.VMEM((32, k), F32),
            pltpu.VMEM((NY - 1, 8, k), F32),
            pltpu.VMEM((NZ, 8, k), F32),
            pltpu.VMEM((k, k), F32),
            dma((NQ,)),
            dma((NQ,)), dma((NQ,)), dma((NQ,)), dma((NQ,)),
            dma((NQ,)), dma((NQ,)), dma((NQ,)), dma((NQ,)),
            dma((9,)), dma((9,)),
        ],
        compiler_params=pltpu.CompilerParams(
            collective_id=0, has_side_effects=True, vmem_limit_bytes=48 << 20
        ),
        cost_estimate=pl.CostEstimate(flops=4 * n * v * k, bytes_accessed=2 * n * v, transcendentals=0),
        name="scores_and_gram",
    )(genotypes, basis_in)


def local(genotypes, basis_in):
    scores, gram = scores_and_gram(genotypes, basis_in)
    lower = jnp.linalg.cholesky(gram)
    new_rows = lax.linalg.triangular_solve(lower, scores.T, left_side=True, lower=True).T
    return (new_rows, lower.T)


def solution(mesh):
    placed = (P("samples", "variants"), P("samples", None))
    return jax.shard_map(
        local, mesh=mesh, in_specs=placed, out_specs=(P("samples", None), P()), check_vma=False
    )
```

time: 743 us -> 159 us (0.21); the launches traced: 733 us -> 159 us
  waiting for transfers between devices: 377 us -> 0 us
  blocking collectives: 256 us -> 0 us
  Pallas kernels: 0 us -> 91.3 us
  between operations: 15.3 us -> 2.09 us
  matrix products: 15 us -> 2.3 us
    psum x2 -> x0, waiting for transfers between devices: 377 us -> none  [the longest x1 254 us: local(): lower = jnp.linalg.cholesky(lax.psum(gram, 'samples'))]
    psum x1 -> x0, blocking collectives: 256 us -> none  [local(): loadings = lax.psum(term, 'samples').astype(jnp.bfloat16)]
    pallas_call x0 -> x1, Pallas kernels: none -> 91.3 us  [scores_and_gram(): pl.pallas_call(functools.partial(comm_kernel, scale, total_samples), out_...]
    dot_general x3 -> x0, matrix products: 9.4 us -> none  [the longest x1 3.36 us: local(): lax.dot_general(genotypes, basis_in, contract, preferred_element_type=jnp...]
  transfers between devices with their start and end apart: 2 -> 0, of which waited for: 2 -> 0; matrix products, arithmetic and copies ran while one was open for 0% -> 0% of each run, Pallas kernels for 0% -> 0%
where the time goes in v1:
time: 159 us
  Pallas kernels  91.3 us (57%)
  other arithmetic  54 us (34%)
  local copies, waits for them, and re-layouts  9.12 us (6%)
  matrix products  2.3 us (1%)
  between operations  2.09 us (1%)
    pallas_call x1, Pallas kernels, scores_and_gram(): pl.pallas_call(functools.partial(comm_kernel, scale, total_samples), out_...  91.3 us
    another operation x6, other arithmetic, local(): lower = jnp.linalg.cholesky(gram)  34.2 us
    another operation x2, other arithmetic, local(): lax.linalg.triangular_solve(lower, scores.T, left_side=True, lower=True)  19.7 us
    unnamed x6, local copies, waits for them, and re-layouts  4.87 us
    another operation x6, local copies, waits for them, and re-layouts  4.02 us

profile of v1, /device:TPU:1, one launch (start us, length us, event | category | flops | bytes accessed | tf_op | source)
XLA Modules:
  0.0 158.9 jit_solution(6426161969459819985)
XLA Ops:
  0.6 0.1 triangular_solve.57
  0.7 0.0 copy-start
  0.7 1.9 %copy-done = bf16[768,2048]{1,0:T(8,128)(2,1)S(1)} copy-done((bf16[768,2048]{1,0:T(8,128)(2,1)S(1)}, bf16[768,2048]{1,0:T(8,128)(2,1)}, u32[]{:S(2)}) %copy-start) | copy-done | bytes 3145752
  2.6 0.0 copy-start.1
  2.6 1.0 copy-done.1
  3.6 91.3 %scores_and_gram.1 = (f32[768,256]{1,0:T(8,128)S(1)}, f32[256,256]{1,0:T(8,128)S(1)}) custom-call(bf16[768,2048]{1,0:T(8,128)(2,1)S(1)} %copy-done, bf16[768,256]{1,0:T(8,128)(2,1)S(1)} %copy-done.1), custom_call_target="tpu_custom_call" | custom-call | flops 1610612736 | bytes 3145728 | tf_op jit(solution)/shard_map/scores_and_gram/pallas_call | solution.py:197
  94.9 0.1 copy.4
  95.1 11.7 %cholesky.50 = f32[128,128]{1,0:T(8,128)S(1)} custom-call(f32[128,128]{1,0:T(8,128)S(1)} %cholesky.118), custom_call_target="Cholesky" | custom-call | tf_op jit(solution)/shard_map/jit(cholesky)/cholesky | solution.py:237
  106.9 9.8 %custom-call.14 = f32[1,128,128]{1,2,0:T(8,128)S(1)} custom-call(f32[1,128,128]{2,1,0:T(8,128)S(1)} %get-tuple-element.31), custom_call_target="InvertDiagBlocksLowerTriangular" | custom-call | tf_op jit(solution)/shard_map/jit(cholesky)/cholesky | solution.py:237
  116.7 0.2 constant_dynamic-update-slice_fusion.1
  116.9 0.3 convolution_subtract_fusion.1
  117.2 11.9 %cholesky.105 = f32[128,128]{1,0:T(8,128)S(1)} custom-call(f32[128,128]{1,0:T(8,128)S(1)} %convolution_subtract_fusion.1), custom_call_target="Cholesky" | custom-call | tf_op jit(solution)/shard_map/jit(cholesky)/cholesky | solution.py:237
  129.1 0.7 compare_reduce_fusion
  131.2 0.8 copy.6
  132.1 4.1 %while.1 = (s32[]{:T(128)}, f32[256,256]{1,0:T(8,128)S(1)}, s32[2,2]{1,0:T(2,128)S(1)}, f32[2,128,128]{2,1,0:T(8,128)S(1)}, s32[]{:T(128)}) while((s32[]{:T(128)}, f32[256,256]{1,0:T(8,128)S(1)}, s32[2,2]{1,0:T(2,128)S(1)}, f32[2,128,128]{2,1,0:T(8,128)S(1)}, s32[]{:T(128)}) %tuple.29), condition=%wide.while_cond, body=%wide.while_body.sunk | while | flops 2 | bytes 131189 | solution.py:238
  132.1 0.7 fusion.16
  132.7 1.3 bitcast_dynamic-update-slice_fusion.2
  134.1 0.7 fusion.16
  134.8 1.3 bitcast_dynamic-update-slice_fusion.2
  136.1 19.7 %custom-call.15 = f32[2,128,128]{1,2,0:T(8,128)S(1)} custom-call(f32[2,128,128]{2,1,0:T(8,128)S(1)} %get-tuple-element.13), custom_call_target="InvertDiagBlocksLowerTriangular" | custom-call | tf_op jit(solution)/shard_map/triangular_solve | solution.py:238
  155.8 0.5 fusion
  156.3 0.8 convolution_subtract_fusion
  157.1 0.5 fusion.6
  157.7 0.1 maximum_bitcast_fusion
  157.7 1.1 copy.5
  (10 shorter events, 0.2 us)
Async XLA Ops:
  0.7 1.9 %copy-start = (bf16[768,2048]{1,0:T(8,128)(2,1)S(1)}, bf16[768,2048]{1,0:T(8,128)(2,1)}, u32[]{:S(2)}) copy-start(bf16[768,2048]{1,0:T(8,128)(2,1)} %g_hbm.1) | copy-start | bytes 9437188
  2.6 1.0 copy-start.1

commit v2 on v1

--- a/solution.py
+++ b/solution.py
@@ -225,18 +225,87 @@
             dma((9,)), dma((9,)),
         ],
         compiler_params=pltpu.CompilerParams(
-            collective_id=0, has_side_effects=True, vmem_limit_bytes=48 << 20
+            collective_id=0, has_side_effects=True, vmem_limit_bytes=60 << 20
         ),
         cost_estimate=pl.CostEstimate(flops=4 * n * v * k, bytes_accessed=2 * n * v, transcendentals=0),
         name="scores_and_gram",
     )(genotypes, basis_in)
 
 
+def eliminate(m, n, panel):
+    rid = lax.broadcasted_iota(jnp.int32, (8, 128), 0)
+    g = [m[8*i:8*i+8] for i in range(n//8)]
+    done = []
+    for j0 in range(0, n, panel):
+        lo = j0//8
+        cols = [[jnp.broadcast_to(g[i][:, j0+k:j0+k+1], (8,128)) for i in range(lo, n//8)] for k in range(panel)]
+        for k in range(panel):
+            j = j0+k
+            v, s = j//8, j%8
+            ck = cols[k]
+            d = ck[v-lo][s:s+1]
+            inv = 1.0/d
+            row = g[v][s:s+1]
+            done.append(row*lax.rsqrt(d))
+            if j == n-1: break
+            keep = rid > s
+            rs = jnp.broadcast_to(row*inv, (8,128))
+            ups = [jnp.broadcast_to(cols[k2][v-lo][s:s+1]*inv, (8,128)) for k2 in range(k+1, panel)]
+            for i in range(v, n//8):
+                c = ck[i-lo]
+                if i == v:
+                    if s == 7: continue
+                    c = jnp.where(keep, c, 0.0)
+                g[i] = g[i] - c*rs
+                for k2 in range(k+1, panel):
+                    cols[k2][i-lo] = cols[k2][i-lo] - c*ups[k2-k-1]
+    return jnp.concatenate(done, axis=0)
+
+
+def chol_body(gram, aug, panel, nb=64):
+    n = gram.shape[0]
+    r, c = (lax.broadcasted_iota(jnp.int32, (n, n), a) for a in (0, 1))
+    aug[:, :n] = gram
+    aug[:, n:] = jnp.where(r == c, 1.0, 0.0)
+    rb, cb = (lax.broadcasted_iota(jnp.int32, (nb, nb), a) for a in (0, 1))
+    eye = jnp.where(rb == cb, 1.0, 0.0)
+    for b in range(n//nb):
+        lo, hi = b*nb, (b+1)*nb
+        m = eliminate(jnp.concatenate([aug[lo:hi, lo:hi], eye], axis=1), nb, panel)
+        v = jnp.where(rb >= cb, m[:, nb:], 0.0)
+        u = jnp.where(rb <= cb, m[:, :nb], 0.0)
+        rest = dot(v, aug[lo:hi, :], ((1,), (0,)), precision=lax.Precision.HIGHEST)
+        aug[lo:hi, :] = rest
+        aug[lo:hi, lo:hi] = u
+        if hi < n:
+            aug[hi:, :] = aug[hi:, :] - dot(rest[:, hi:n], rest, ((0,), (0,)), precision=lax.Precision.HIGHEST)
+
+
+def factor_kernel(panel, gram, scores, basis, factor, aug):
+    n = gram.shape[0]
+    chol_body(gram[...], aug, panel)
+    r, c = (lax.broadcasted_iota(jnp.int32, (n, n), a) for a in (0, 1))
+    factor[...] = jnp.where(r <= c, aug[:, :n], 0.0)
+    basis[...] = dot(scores[...], jnp.where(r >= c, aug[:, n:], 0.0), ((1,), (1,)), precision=lax.Precision.HIGHEST)
+
+
+def factor_and_basis(gram, scores):
+    k = gram.shape[0]
+    vmem = pl.BlockSpec(memory_space=pltpu.VMEM)
+    return pl.pallas_call(
+        functools.partial(factor_kernel, 8),
+        out_shape=[jax.ShapeDtypeStruct(scores.shape, F32), jax.ShapeDtypeStruct(gram.shape, F32)],
+        in_specs=[vmem, vmem],
+        out_specs=[vmem, vmem],
+        scratch_shapes=[pltpu.VMEM((k, 2 * k), F32)],
+        compiler_params=pltpu.CompilerParams(vmem_limit_bytes=40 << 20),
+        name="factor_and_basis",
+    )(gram, scores)
+
+
 def local(genotypes, basis_in):
     scores, gram = scores_and_gram(genotypes, basis_in)
-    lower = jnp.linalg.cholesky(gram)
-    new_rows = lax.linalg.triangular_solve(lower, scores.T, left_side=True, lower=True).T
-    return (new_rows, lower.T)
+    return tuple(factor_and_basis(gram, scores))
 
 
 def solution(mesh):

time: 159 us -> 107 us (0.67)
  other arithmetic: 54 us -> 0 us
  Pallas kernels: 91.3 us -> 104 us
  local copies, waits for them, and re-layouts: 9.12 us -> 2.08 us
  matrix products: 2.3 us -> 0 us
    another operation x8 -> x0, other arithmetic: 53.9 us -> none  [the longest x6 34.2 us: local(): lower = jnp.linalg.cholesky(gram)]
    pallas_call x0 -> x1, Pallas kernels: none -> 10.3 us  [factor_and_basis(): pl.pallas_call(functools.partial(factor_kernel, 8), out_shape=[jax.ShapeD...]
    another operation x9 -> x0, local copies, waits for them, and re-layouts: 4.12 us -> none
    unnamed x6 -> x4, local copies, waits for them, and re-layouts: 4.87 us -> 2.08 us
    another operation x5 -> x0, matrix products: 2.3 us -> none  [the longest x3 1.83 us: local(): lax.linalg.triangular_solve(lower, scores.T, left_side=True, lower=True)]
    pallas_call x1, Pallas kernels: 91.3 us -> 93.6 us  [scores_and_gram(): pl.pallas_call(functools.partial(comm_kernel, scale, total_samples), out_...]
where the time goes in v2:
time: 107 us
  Pallas kernels  104 us (97%)
  local copies, waits for them, and re-layouts  2.08 us (2%)
    pallas_call x1, Pallas kernels, scores_and_gram(): pl.pallas_call(functools.partial(comm_kernel, scale, total_samples), out_...  93.6 us
    pallas_call x1, Pallas kernels, factor_and_basis(): pl.pallas_call(functools.partial(factor_kernel, 8), out_shape=[jax.ShapeD...  10.3 us

profile of v2, /device:TPU:1, one launch (start us, length us, event | category | flops | bytes accessed | tf_op | source)
XLA Modules:
  0.0 106.6 jit_solution(17223119705762809090)
XLA Ops:
  0.6 93.6 %scores_and_gram.1 = (f32[768,256]{1,0:T(8,128)}, f32[256,256]{1,0:T(8,128)}) custom-call(bf16[768,2048]{1,0:T(8,128)(2,1)} %g_hbm.1, bf16[768,256]{1,0:T(8,128)(2,1)} %b_ref.1), custom_call_target="tpu_custom_call" | custom-call | flops 1610612736 | bytes 3145728 | tf_op jit(solution)/shard_map/scores_and_gram/pallas_call | solution.py:197
  94.2 0.0 copy-start
  94.3 1.1 %copy-done = f32[768,256]{1,0:T(8,128)S(1)} copy-done((f32[768,256]{1,0:T(8,128)S(1)}, f32[768,256]{1,0:T(8,128)}, u32[]{:S(2)}) %copy-start) | copy-done | bytes 786456
  95.4 0.0 copy-start.1
  95.4 0.9 copy-done.1
  96.3 10.3 %factor_and_basis.1 = (f32[768,256]{1,0:T(8,128)}, f32[256,256]{1,0:T(8,128)}) custom-call(f32[256,256]{1,0:T(8,128)S(1)} %copy-done.1, f32[768,256]{1,0:T(8,128)S(1)} %copy-done), custom_call_target="tpu_custom_call" | custom-call | tf_op jit(solution)/shard_map/factor_and_basis/pallas_call | solution.py:295
Async XLA Ops:
  94.2 1.1 %copy-start = (f32[768,256]{1,0:T(8,128)S(1)}, f32[768,256]{1,0:T(8,128)}, u32[]{:S(2)}) copy-start(f32[768,256]{1,0:T(8,128)} %get-tuple-element.5.scores) | copy-start | bytes 2359300
  95.4 0.9 copy-start.1

commit v3 on v1

v3 whole, which is shorter than its diff:
```python
import functools

import jax
import jax.numpy as jnp
from jax import lax
from jax.experimental import pallas as pl
from jax.experimental.pallas import tpu as pltpu
from jax.sharding import PartitionSpec as P

MESH = pl.DeviceIdType.MESH
NZ, NY, NX, NC = 16, 4, 4, 2
NQ = 4
F32, BF16 = jnp.float32, jnp.bfloat16
SHIFT = 4096.0
LOG_SHIFT = 8.317766166719343
WIDE_SHIFT = 16384.0
LOG_WIDE_SHIFT = 9.704060527839234


def encode(x):
    s = x * SHIFT
    s2 = s * s
    return (s2 * s2 * s).astype(BF16)


def decode(y):
    y = y.astype(F32)
    r = jnp.exp(jnp.log(jnp.abs(y)) * 0.2 - LOG_SHIFT)
    return jnp.where(y < 0, -r, r)


def encode_wide(x):
    s = x * WIDE_SHIFT
    return (s * s * s).astype(BF16)


def decode_wide(y):
    y = y.astype(F32)
    r = jnp.exp(jnp.log(jnp.abs(y)) * (1.0 / 3.0) - LOG_WIDE_SHIFT)
    return jnp.where(y < 0, -r, r)


def hops(d, n):
    return min(d, n - d)


def dot(a, b, dims, **kw):
    return lax.dot_general(a, b, (dims, ((), ())), preferred_element_type=F32, **kw)


def comm_kernel(
    scale, total, g_hbm, b_hbm, scores_ref, gram_ref,
    bbuf, gbuf, tf, ysend, yrecv, sf, zsend, zrecv, lall,
    spart, crecv, xsend, xrecv, sall, gp, gprecv, gzall,
    load_sem, out_sem, ys, yr, zs, zr, ls, lr, us, ur, ps, pr,
):
    samp, var = lax.axis_index("samples"), lax.axis_index("variants")
    z, y = lax.div(samp, NY), lax.rem(samp, NY)
    x, c = lax.div(var, NC), lax.rem(var, NC)

    def dev(dz, dy, dx, dc):
        return (
            lax.rem(z + dz, NZ) * NY + lax.rem(y + dy, NY),
            lax.rem(x + dx, NX) * NC + lax.rem(c + dc, NC),
        )

    def start(src, dst, send, recv, to):
        pltpu.make_async_remote_copy(
            src_ref=src, dst_ref=dst, send_sem=send, recv_sem=recv,
            device_id=to, device_id_type=MESH,
        ).start()

    def wait(ref, sem):
        pltpu.make_async_copy(ref, ref, sem).wait()

    def rows(i, n):
        return pl.ds(pl.multiple_of(i * n, n), n)

    plane = [(dy, dx, dc) for dy in range(NY) for dx in range(NX) for dc in range(NC)][1:]
    plane.sort(key=lambda p: -hops(p[0], NY) - hops(p[1], NX))
    far = sorted(range(1, NZ), key=lambda d: -hops(d, NZ))
    partners = [(dz, 0, 0, 0) for dz in far] + [(0,) + p for p in plane]

    cols = gbuf.shape[2]
    loads = [
        pltpu.make_async_copy(g_hbm.at[:, pl.ds(q * cols, cols)], gbuf.at[q], load_sem.at[q])
        for q in range(NQ)
    ]
    load_b = pltpu.make_async_copy(b_hbm, bbuf, load_sem.at[NQ])
    load_b.start()
    for load in loads:
        load.start()
    barrier = pltpu.get_barrier_semaphore()
    for p in partners:
        pl.semaphore_signal(barrier, inc=1, device_id=dev(*p), device_id_type=MESH)

    def term(q):
        loads[q].wait()
        t = dot(bbuf[...], gbuf[q], ((0,), (0,)))
        for i in range(NY):
            tf[q, i] = t[:, i * 128:(i + 1) * 128]

    def send_y(q):
        for dy in range(1, NY):
            to = lax.rem(y + dy, NY)
            ysend[q, dy - 1] = encode(tf[q, to])
            start(ysend.at[q, dy - 1], yrecv.at[q, dy - 1], ys.at[q], yr.at[q], dev(0, dy, 0, 0))

    load_b.wait()
    term(0)
    pl.semaphore_wait(barrier, len(partners))
    send_y(0)
    for q in range(1, NQ):
        term(q)
        send_y(q)
    for q in range(NQ):
        wait(yrecv.at[q], yr.at[q])
        s = tf[q, y]
        for i in range(NY - 1):
            s = s + decode(yrecv[q, i])
        sf[q] = s
        zsend[q] = encode(s)
        for dz in far:
            to = lax.rem(z + dz, NZ)
            start(zsend.at[q, rows(to, 16)], zrecv.at[q, pl.ds((dz - 1) * 16, 16)], zs.at[q], zr.at[q], dev(dz, 0, 0, 0))
    for q in range(NQ):
        wait(zrecv.at[q], zr.at[q])
        s = sf[q, rows(z, 16)]
        for i in range(NZ - 1):
            s = s + decode(zrecv[q, i * 16:(i + 1) * 16])
        lall[q, y, rows(z, 16)] = s.astype(BF16)
        for dz in far:
            mine = lall.at[q, y, rows(z, 16)]
            start(mine, mine, ls.at[q], lr.at[q], dev(dz, 0, 0, 0))
    for q in range(NQ):
        wait(lall.at[q, y, pl.ds(0, 240)], lr.at[q])
        for dy in range(1, NY):
            mine = lall.at[q, y]
            start(mine, mine, us.at[q], ur.at[q], dev(0, dy, 0, 0))
    for q in range(NQ):
        wait(lall.at[q, pl.ds(0, 3)], ur.at[q])
        part = jnp.concatenate([lall[q, i] for i in range(NY)], axis=1)
        t = dot(gbuf[q], part, ((1,), (1,)))
        if q == 0:
            spart[...] = t
        else:
            spart[...] += t
    half, chunk = spart.shape[0] // NC, spart.shape[0] // (NC * NX)
    other = lax.rem(c + 1, NC)
    start(spart.at[rows(other, half)], crecv, ps.at[0], pr.at[0], dev(0, 0, 0, 1))
    wait(crecv, pr.at[0])
    crecv[...] = crecv[...] + spart[rows(c, half)]
    xsend[...] = encode_wide(crecv[...])
    for dx in (2, 1, 3):
        to = lax.rem(x + dx, NX)
        start(xsend.at[rows(to, chunk)], xrecv.at[dx - 1], ps.at[1], pr.at[1], dev(0, 0, dx, 0))
    wait(xrecv, pr.at[1])
    r = crecv[rows(x, chunk)]
    for i in range(NX - 1):
        r = r + decode_wide(xrecv[i])
    r = r * scale
    mine = c * NX + x
    sall[rows(mine, chunk)] = r
    gp[...] = dot(r, r, ((0,), (0,)), precision=lax.Precision.HIGHEST) * (1.0 / total)
    for i, (dy, dx, dc) in enumerate(plane):
        to = (lax.rem(c + dc, NC) * NX + lax.rem(x + dx, NX)) * NY + lax.rem(y + dy, NY)
        start(gp.at[rows(to, 8)], gprecv.at[i], ps.at[2], pr.at[2], dev(0, dy, dx, dc))
    for dx in (2, 1, 3):
        own = sall.at[rows(mine, chunk)]
        start(own, own, ps.at[4], pr.at[4], dev(0, 0, dx, 0))
    wait(gprecv, pr.at[2])
    spot = (c * NX + x) * NY + y
    s = gp[rows(spot, 8)]
    for i in range(len(plane)):
        s = s + gprecv[i]
    gzall[z] = s
    for dz in far:
        start(gzall.at[z], gzall.at[z], ps.at[6], pr.at[6], dev(dz, 0, 0, 0))
    wait(sall.at[pl.ds(0, 3 * chunk)], pr.at[4])
    own = sall.at[rows(c, half)]
    start(own, own, ps.at[7], pr.at[7], dev(0, 0, 0, 1))
    keep = pltpu.make_async_copy(own, scores_ref.at[rows(c, half)], out_sem.at[0])
    keep.start()
    wait(sall.at[pl.ds(0, half)], pr.at[7])
    own = sall.at[rows(other, half)]
    keep2 = pltpu.make_async_copy(own, scores_ref.at[rows(other, half)], out_sem.at[1])
    keep2.start()
    wait(gzall.at[pl.ds(0, NZ - 1)], pr.at[6])
    s = gzall[0]
    for i in range(1, NZ):
        s = s + gzall[i]
    own = gram_ref.at[rows(spot, 8)]
    own[...] = s
    for p in plane:
        start(own, own, ps.at[8], pr.at[8], dev(0, *p))
    keep.wait()
    keep2.wait()
    wait(gram_ref.at[pl.ds(0, 248)], pr.at[8])
    for q in range(NQ):
        wait(ysend.at[q], ys.at[q])
        wait(zrecv.at[q], zs.at[q])
        wait(zrecv.at[q], ls.at[q])
        wait(lall.at[q, pl.ds(0, 3)], us.at[q])
    wait(crecv, ps.at[0])
    wait(xrecv, ps.at[1])
    wait(gprecv, ps.at[2])
    wait(sall.at[pl.ds(0, 3 * chunk)], ps.at[4])
    wait(gzall.at[pl.ds(0, NZ - 1)], ps.at[6])
    wait(sall.at[pl.ds(0, half)], ps.at[7])
    wait(gram_ref.at[pl.ds(0, 248)], ps.at[8])


def scores_and_gram(genotypes, basis_in):
    n, v = genotypes.shape
    k = basis_in.shape[1]
    total_samples = n * lax.axis_size("samples")
    scale = 1.0 / (v * lax.axis_size("variants")) ** 0.5
    part = v // NQ
    chunk = n // (NC * NX)
    dma = pltpu.SemaphoreType.DMA
    vmem = pl.BlockSpec(memory_space=pltpu.VMEM)
    return pl.pallas_call(
        functools.partial(comm_kernel, scale, total_samples),
        out_shape=[jax.ShapeDtypeStruct((n, k), F32), jax.ShapeDtypeStruct((k, k), F32)],
        in_specs=[pl.BlockSpec(memory_space=pl.ANY)] * 2,
        out_specs=[pl.BlockSpec(memory_space=pl.ANY), vmem],
        scratch_shapes=[
            pltpu.VMEM((n, k), BF16),
            pltpu.VMEM((NQ, n, part), BF16),
            pltpu.VMEM((NQ, NY, k, 128), F32),
            pltpu.VMEM((NQ, NY - 1, k, 128), BF16),
            pltpu.VMEM((NQ, NY - 1, k, 128), BF16),
            pltpu.VMEM((NQ, k, 128), F32),
            pltpu.VMEM((NQ, k, 128), BF16),
            pltpu.VMEM((NQ, (NZ - 1) * 16, 128), BF16),
            pltpu.VMEM((NQ, NY, k, 128), BF16),
            pltpu.VMEM((n, k), F32),
            pltpu.VMEM((n // NC, k), F32),
            pltpu.VMEM((n // NC, k), BF16),
            pltpu.VMEM((NX - 1, chunk, k), BF16),
            pltpu.VMEM((n, k), F32),
            pltpu.VMEM((k, k), F32),
            pltpu.VMEM((NX * NY * NC - 1, 8, k), F32),
            pltpu.VMEM((NZ, 8, k), F32),
            dma((NQ + 1,)), dma((2,)),
            dma((NQ,)), dma((NQ,)), dma((NQ,)), dma((NQ,)),
            dma((NQ,)), dma((NQ,)), dma((NQ,)), dma((NQ,)),
            dma((9,)), dma((9,)),
        ],
        compiler_params=pltpu.CompilerParams(
            collective_id=0, has_side_effects=True, vmem_limit_bytes=24 << 20
        ),
        cost_estimate=pl.CostEstimate(flops=4 * n * v * k, bytes_accessed=2 * n * v, transcendentals=0),
        name="scores_and_gram",
    )(*(pltpu.with_memory_space_constraint(a, pltpu.HBM) for a in (genotypes, basis_in)))


def eliminate(a, panel):
    n = a.shape[0]
    row, col = (lax.broadcasted_iota(jnp.int32, (n, n), i) for i in (0, 1))
    eye = jnp.where(row == col, 1.0, 0.0)
    sub = lax.broadcasted_iota(jnp.int32, (8, n), 0)
    left = [a[8 * i:8 * i + 8] for i in range(n // 8)]
    right = [eye[8 * i:8 * i + 8] for i in range(n // 8)]
    upper, inverse = [], []
    for j0 in range(0, n, panel):
        lo = j0 // 8
        cols = [
            [jnp.broadcast_to(g[:, j0 + k:j0 + k + 1], (8, n)) for g in left[lo:]]
            for k in range(panel)
        ]
        for k in range(panel):
            j = j0 + k
            v, s = j // 8, j % 8
            pivot = cols[k][v - lo][s:s + 1]
            inv = 1.0 / pivot
            root = lax.rsqrt(pivot)
            ra, rb = left[v][s:s + 1], right[v][s:s + 1]
            upper.append(ra * root)
            inverse.append(rb * root)
            if j == n - 1:
                break
            sa = jnp.broadcast_to(ra * inv, (8, n))
            sb = jnp.broadcast_to(rb * inv, (8, n))
            sc = [jnp.broadcast_to(cols[m][v - lo][s:s + 1] * inv, (8, n)) for m in range(k + 1, panel)]
            for i in range(v if s < 7 else v + 1, n // 8):
                c = cols[k][i - lo]
                if i == v:
                    c = jnp.where(sub > s, c, 0.0)
                left[i] = left[i] - c * sa
                right[i] = right[i] - c * sb
                for m in range(k + 1, panel):
                    cols[m][i - lo] = cols[m][i - lo] - c * sc[m - k - 1]
    upper = jnp.where(row <= col, jnp.concatenate(upper, axis=0), 0.0)
    inverse = jnp.where(row >= col, jnp.concatenate(inverse, axis=0), 0.0)
    return upper, inverse


def split(a):
    high = a.astype(BF16)
    return high, (a - high.astype(F32)).astype(BF16)


def dot3(a, b, dims):
    (ah, al), (bh, bl) = split(a), split(b)
    return dot(ah, bh, dims) + (dot(ah, bl, dims) + dot(al, bh, dims))


def factor_kernel(panel, gram, scores_hbm, basis_hbm, factor, scores, basis, sems):
    n = gram.shape[0]
    h = n // 2
    load = pltpu.make_async_copy(scores_hbm, scores, sems.at[0])
    load.start()
    u11, v1 = eliminate(gram[:h, :h], panel)
    load.wait()
    u12 = dot(v1, gram[:h, h:], ((1,), (0,)), precision=lax.Precision.HIGHEST)
    a22 = gram[h:, h:] - dot(u12, u12, ((0,), (0,)), precision=lax.Precision.HIGHEST)
    first = dot3(scores[:, :h], v1, ((1,), (1,)))
    rest = scores[:, h:] - dot3(first, u12, ((1,), (0,)))
    u22, v2 = eliminate(a22, panel)
    basis[0] = first
    basis[1] = dot3(rest, v2, ((1,), (1,)))
    out1 = pltpu.make_async_copy(basis.at[0], basis_hbm.at[:, pl.ds(0, h)], sems.at[1])
    out1.start()
    out2 = pltpu.make_async_copy(basis.at[1], basis_hbm.at[:, pl.ds(h, h)], sems.at[2])
    out2.start()
    factor[:h, :h] = u11
    factor[:h, h:] = u12
    factor[h:, :h] = jnp.zeros((h, h), F32)
    factor[h:, h:] = u22
    out1.wait()
    out2.wait()


def factor_and_basis(gram, scores):
    n, k = scores.shape
    vmem, hbm = pl.BlockSpec(memory_space=pltpu.VMEM), pl.BlockSpec(memory_space=pltpu.HBM)
    return pl.pallas_call(
        functools.partial(factor_kernel, 8),
        out_shape=[jax.ShapeDtypeStruct(scores.shape, F32), jax.ShapeDtypeStruct(gram.shape, F32)],
        in_specs=[vmem, hbm],
        out_specs=[hbm, vmem],
        scratch_shapes=[
            pltpu.VMEM((n, k), F32),
            pltpu.VMEM((2, n, k // 2), F32),
            pltpu.SemaphoreType.DMA((3,)),
        ],
        compiler_params=pltpu.CompilerParams(vmem_limit_bytes=40 << 20),
        name="factor_and_basis",
    )(gram, scores)


def local(genotypes, basis_in):
    scores, gram = scores_and_gram(genotypes, basis_in)
    return tuple(factor_and_basis(gram, scores))


def solution(mesh):
    placed = (P("samples", "variants"), P("samples", None))
    return jax.shard_map(
        local, mesh=mesh, in_specs=placed, out_specs=(P("samples", None), P()), check_vma=False
    )
```

time: 159 us -> 92.4 us (0.58)
  other arithmetic: 54 us -> 0 us
  local copies, waits for them, and re-layouts: 9.12 us -> 0 us
  matrix products: 2.3 us -> 0 us
    another operation x8 -> x0, other arithmetic: 53.9 us -> none  [the longest x6 34.2 us: local(): lower = jnp.linalg.cholesky(gram)]
    pallas_call x0 -> x1, Pallas kernels: none -> 9.37 us  [factor_and_basis(): pl.pallas_call(functools.partial(factor_kernel, 8), out_shape=[jax.ShapeD...]
    pallas_call x1, Pallas kernels: 91.3 us -> 82.2 us  [scores_and_gram(): pl.pallas_call(functools.partial(comm_kernel, scale, total_samples), out_...]
    unnamed x6 -> x0, local copies, waits for them, and re-layouts: 4.87 us -> none
    another operation x9 -> x0, local copies, waits for them, and re-layouts: 4.12 us -> none
    another operation x5 -> x0, matrix products: 2.3 us -> none  [the longest x3 1.83 us: local(): lax.linalg.triangular_solve(lower, scores.T, left_side=True, lower=True)]
where the time goes in v3:
time: 92.4 us; the launch traced here: 92.2 us
  Pallas kernels  91.6 us (99%)
    pallas_call x1, Pallas kernels, scores_and_gram(): pl.pallas_call(functools.partial(comm_kernel, scale, total_samples), out_...  82.2 us
    pallas_call x1, Pallas kernels, factor_and_basis(): pl.pallas_call(functools.partial(factor_kernel, 8), out_shape=[jax.ShapeD...  9.37 us

profile of v3, /device:TPU:1, one launch (start us, length us, event | category | flops | bytes accessed | tf_op | source)
XLA Modules:
  0.0 92.2 jit_solution(5096844937424883141)
XLA Ops:
  0.6 82.2 %scores_and_gram.1 = (f32[768,256]{1,0:T(8,128)S(1)}, f32[256,256]{1,0:T(8,128)S(1)}) custom-call(bf16[768,2048]{1,0:T(8,128)(2,1)} %g_hbm.1, bf16[768,256]{1,0:T(8,128)(2,1)} %b_hbm.1), custom_call_target="tpu_custom_call" | custom-call | flops 1610612736 | bytes 3145728 | tf_op jit(solution)/shard_map/scores_and_gram/pallas_call | solution.py:222
  82.9 9.4 %factor_and_basis.1 = (f32[768,256]{1,0:T(8,128)}, f32[256,256]{1,0:T(8,128)}) custom-call(f32[256,256]{1,0:T(8,128)S(1)} %get-tuple-element.4.gram, f32[768,256]{1,0:T(8,128)S(1)} %get-tuple-element.5.scores_hbm), custom_call_target="tpu_custom_call" | custom-call | tf_op jit(solution)/shard_map/factor_and_basis/pallas_call | solution.py:338

commit v4 on v3

--- a/solution.py
+++ b/solution.py
@@ -52,11 +52,12 @@
     scale, total, g_hbm, b_hbm, scores_ref, gram_ref,
     bbuf, gbuf, tf, ysend, yrecv, sf, zsend, zrecv, lall,
     spart, crecv, xsend, xrecv, sall, gp, gprecv, gzall,
-    load_sem, out_sem, ys, yr, zs, zr, ls, lr, us, ur, ps, pr,
+    load_sem, out_sem, known, ys, yr, zs, zr, ls, lr, us, ur, cs, cr, xs, xr, ps, pr,
 ):
     samp, var = lax.axis_index("samples"), lax.axis_index("variants")
     z, y = lax.div(samp, NY), lax.rem(samp, NY)
     x, c = lax.div(var, NC), lax.rem(var, NC)
+    odd = lax.rem(z, 2)
 
     def dev(dz, dy, dx, dc):
         return (
@@ -73,26 +74,31 @@
     def wait(ref, sem):
         pltpu.make_async_copy(ref, ref, sem).wait()
 
+    def signal(sem, to):
+        pl.semaphore_signal(sem, inc=1, device_id=to, device_id_type=MESH)
+
     def rows(i, n):
         return pl.ds(pl.multiple_of(i * n, n), n)
 
     plane = [(dy, dx, dc) for dy in range(NY) for dx in range(NX) for dc in range(NC)][1:]
     plane.sort(key=lambda p: -hops(p[0], NY) - hops(p[1], NX))
     far = sorted(range(1, NZ), key=lambda d: -hops(d, NZ))
-    partners = [(dz, 0, 0, 0) for dz in far] + [(0,) + p for p in plane]
-
+    near = [(dz, 0, 0, 0) for dz in (2, 14, 1, 15)] + [(0, dy, 0, 0) for dy in (2, 1, 3)]
+    near += [(0, 0, dx, 0) for dx in (2, 1, 3)] + [(0, 0, 0, 1)]
+    units = [(q, h) for q in range(NQ) for h in range(2)]
+
+    load_b = pltpu.make_async_copy(b_hbm, bbuf, load_sem.at[NQ])
+    load_b.start()
     cols = gbuf.shape[2]
     loads = [
         pltpu.make_async_copy(g_hbm.at[:, pl.ds(q * cols, cols)], gbuf.at[q], load_sem.at[q])
         for q in range(NQ)
     ]
-    load_b = pltpu.make_async_copy(b_hbm, bbuf, load_sem.at[NQ])
-    load_b.start()
     for load in loads:
         load.start()
     barrier = pltpu.get_barrier_semaphore()
-    for p in partners:
-        pl.semaphore_signal(barrier, inc=1, device_id=dev(*p), device_id_type=MESH)
+    for p in near:
+        signal(barrier, dev(*p))
 
     def term(q):
         loads[q].wait()
@@ -101,65 +107,97 @@
             tf[q, i] = t[:, i * 128:(i + 1) * 128]
 
     def send_y(q):
-        for dy in range(1, NY):
-            to = lax.rem(y + dy, NY)
-            ysend[q, dy - 1] = encode(tf[q, to])
-            start(ysend.at[q, dy - 1], yrecv.at[q, dy - 1], ys.at[q], yr.at[q], dev(0, dy, 0, 0))
+        for h in range(2):
+            for dy in (2, 1, 3):
+                to = lax.rem(y + dy, NY)
+                ysend[q, h, dy - 1] = encode(tf[q, to, h * 128:(h + 1) * 128])
+                start(ysend.at[q, h, dy - 1], yrecv.at[q, h, dy - 1], ys.at[q], yr.at[q, h], dev(0, dy, 0, 0))
 
     load_b.wait()
     term(0)
-    pl.semaphore_wait(barrier, len(partners))
+    pl.semaphore_wait(barrier, len(near))
+    for dz in (2, 14):
+        signal(known.at[0], dev(dz, 0, 0, 0))
     send_y(0)
-    for q in range(1, NQ):
+    term(1)
+    send_y(1)
+    pl.semaphore_wait(known.at[0], 2)
+    for dz in (4, 12):
+        signal(known.at[1], dev(dz, 0, 0, 0))
+    for q in range(2, NQ):
         term(q)
         send_y(q)
-    for q in range(NQ):
-        wait(yrecv.at[q], yr.at[q])
-        s = tf[q, y]
+    pl.semaphore_wait(known.at[1], 2)
+    for q, h in units:
+        wait(yrecv.at[q, h], yr.at[q, h])
+        s = tf[q, y, h * 128:(h + 1) * 128]
         for i in range(NY - 1):
-            s = s + decode(yrecv[q, i])
-        sf[q] = s
-        zsend[q] = encode(s)
-        for dz in far:
-            to = lax.rem(z + dz, NZ)
-            start(zsend.at[q, rows(to, 16)], zrecv.at[q, pl.ds((dz - 1) * 16, 16)], zs.at[q], zr.at[q], dev(dz, 0, 0, 0))
+            s = s + decode(yrecv[q, h, i])
+        sf[q, h] = s
+        zsend[q, h] = encode(s)
+        par = lax.rem(z + h, 2)
+        for i in (4, 3, 5, 2, 6, 1, 7, 0):
+            def send_tile(i=i):
+                d = 2 * i + par
+                to = lax.rem(z + d, NZ)
+                start(
+                    zsend.at[q, h, rows(lax.div(to, 2), 16)], zrecv.at[q, rows(d - 1, 16)],
+                    zs.at[q], zr.at[q], dev(d, 0, 0, 0),
+                )
+            if i:
+                send_tile()
+            else:
+                pl.when(par == 1)(send_tile)
+    tile = odd * 8 + lax.div(z, 2)
     for q in range(NQ):
         wait(zrecv.at[q], zr.at[q])
-        s = sf[q, rows(z, 16)]
+        s = sf[q, odd, rows(lax.div(z, 2), 16)]
         for i in range(NZ - 1):
             s = s + decode(zrecv[q, i * 16:(i + 1) * 16])
-        lall[q, y, rows(z, 16)] = s.astype(BF16)
+        lall[q, y, rows(tile, 16)] = s.astype(BF16)
         for dz in far:
-            mine = lall.at[q, y, rows(z, 16)]
-            start(mine, mine, ls.at[q], lr.at[q], dev(dz, 0, 0, 0))
-    for q in range(NQ):
-        wait(lall.at[q, y, pl.ds(0, 240)], lr.at[q])
-        for dy in range(1, NY):
-            mine = lall.at[q, y]
-            start(mine, mine, us.at[q], ur.at[q], dev(0, dy, 0, 0))
-    for q in range(NQ):
-        wait(lall.at[q, pl.ds(0, 3)], ur.at[q])
-        part = jnp.concatenate([lall[q, i] for i in range(NY)], axis=1)
+            mine = lall.at[q, y, rows(tile, 16)]
+            start(mine, mine, ls.at[q], lr.at[q, odd], dev(dz, 0, 0, 0))
+    for q, h in units:
+        @pl.when(odd == h)
+        def _():
+            wait(lall.at[q, y, pl.ds(0, 112)], lr.at[q, h])
+
+        @pl.when(odd != h)
+        def _():
+            wait(lall.at[q, y, pl.ds(0, 128)], lr.at[q, h])
+
+        for dy in (2, 1, 3):
+            mine = lall.at[q, y, pl.ds(h * 128, 128)]
+            start(mine, mine, us.at[q], ur.at[q, h], dev(0, dy, 0, 0))
+    half, chunk = spart.shape[1] // NC, spart.shape[1] // (NC * NX)
+    other = lax.rem(c + 1, NC)
+    for q, h in units:
+        wait(yrecv.at[q, h], ur.at[q, h])
+        part = jnp.concatenate([lall[q, i, h * 128:(h + 1) * 128] for i in range(NY)], axis=1)
         t = dot(gbuf[q], part, ((1,), (1,)))
         if q == 0:
-            spart[...] = t
+            spart[h] = t
         else:
-            spart[...] += t
-    half, chunk = spart.shape[0] // NC, spart.shape[0] // (NC * NX)
-    other = lax.rem(c + 1, NC)
-    start(spart.at[rows(other, half)], crecv, ps.at[0], pr.at[0], dev(0, 0, 0, 1))
-    wait(crecv, pr.at[0])
-    crecv[...] = crecv[...] + spart[rows(c, half)]
-    xsend[...] = encode_wide(crecv[...])
-    for dx in (2, 1, 3):
-        to = lax.rem(x + dx, NX)
-        start(xsend.at[rows(to, chunk)], xrecv.at[dx - 1], ps.at[1], pr.at[1], dev(0, 0, dx, 0))
-    wait(xrecv, pr.at[1])
-    r = crecv[rows(x, chunk)]
-    for i in range(NX - 1):
-        r = r + decode_wide(xrecv[i])
-    r = r * scale
+            spart[h] += t
+        if q == NQ - 1:
+            start(spart.at[h, rows(other, half)], crecv.at[h], cs.at[h], cr.at[h], dev(0, 0, 0, 1))
+    for h in range(2):
+        wait(crecv.at[h], cr.at[h])
+        crecv[h] = crecv[h] + spart[h, rows(c, half)]
+        xsend[h] = encode_wide(crecv[h])
+        for dx in (2, 1, 3):
+            to = lax.rem(x + dx, NX)
+            start(xsend.at[h, rows(to, chunk)], xrecv.at[h, dx - 1], xs.at[h], xr.at[h], dev(0, 0, dx, 0))
     mine = c * NX + x
+    r = []
+    for h in range(2):
+        wait(xrecv.at[h], xr.at[h])
+        s = crecv[h, rows(x, chunk)]
+        for i in range(NX - 1):
+            s = s + decode_wide(xrecv[h, i])
+        r.append(s * scale)
+    r = jnp.concatenate(r, axis=1)
     sall[rows(mine, chunk)] = r
     gp[...] = dot(r, r, ((0,), (0,)), precision=lax.Precision.HIGHEST) * (1.0 / total)
     for i, (dy, dx, dc) in enumerate(plane):
@@ -201,8 +239,9 @@
         wait(zrecv.at[q], zs.at[q])
         wait(zrecv.at[q], ls.at[q])
         wait(lall.at[q, pl.ds(0, 3)], us.at[q])
-    wait(crecv, ps.at[0])
-    wait(xrecv, ps.at[1])
+    for h in range(2):
+        wait(crecv.at[h], cs.at[h])
+        wait(xrecv.at[h], xs.at[h])
     wait(gprecv, ps.at[2])
     wait(sall.at[pl.ds(0, 3 * chunk)], ps.at[4])
     wait(gzall.at[pl.ds(0, NZ - 1)], ps.at[6])
@@ -228,23 +267,24 @@
             pltpu.VMEM((n, k), BF16),
             pltpu.VMEM((NQ, n, part), BF16),
             pltpu.VMEM((NQ, NY, k, 128), F32),
-            pltpu.VMEM((NQ, NY - 1, k, 128), BF16),
-            pltpu.VMEM((NQ, NY - 1, k, 128), BF16),
-            pltpu.VMEM((NQ, k, 128), F32),
-            pltpu.VMEM((NQ, k, 128), BF16),
+            pltpu.VMEM((NQ, 2, NY - 1, k // 2, 128), BF16),
+            pltpu.VMEM((NQ, 2, NY - 1, k // 2, 128), BF16),
+            pltpu.VMEM((NQ, 2, k // 2, 128), F32),
+            pltpu.VMEM((NQ, 2, k // 2, 128), BF16),
             pltpu.VMEM((NQ, (NZ - 1) * 16, 128), BF16),
             pltpu.VMEM((NQ, NY, k, 128), BF16),
-            pltpu.VMEM((n, k), F32),
-            pltpu.VMEM((n // NC, k), F32),
-            pltpu.VMEM((n // NC, k), BF16),
-            pltpu.VMEM((NX - 1, chunk, k), BF16),
+            pltpu.VMEM((2, n, k // 2), F32),
+            pltpu.VMEM((2, n // NC, k // 2), F32),
+            pltpu.VMEM((2, n // NC, k // 2), BF16),
+            pltpu.VMEM((2, NX - 1, chunk, k // 2), BF16),
             pltpu.VMEM((n, k), F32),
             pltpu.VMEM((k, k), F32),
             pltpu.VMEM((NX * NY * NC - 1, 8, k), F32),
             pltpu.VMEM((NZ, 8, k), F32),
-            dma((NQ + 1,)), dma((2,)),
-            dma((NQ,)), dma((NQ,)), dma((NQ,)), dma((NQ,)),
-            dma((NQ,)), dma((NQ,)), dma((NQ,)), dma((NQ,)),
+            dma((NQ + 1,)), dma((2,)), pltpu.SemaphoreType.REGULAR((2,)),
+            dma((NQ,)), dma((NQ, 2)), dma((NQ,)), dma((NQ,)),
+            dma((NQ,)), dma((NQ, 2)), dma((NQ,)), dma((NQ, 2)),
+            dma((2,)), dma((2,)), dma((2,)), dma((2,)),
             dma((9,)), dma((9,)),
         ],
         compiler_params=pltpu.CompilerParams(

time: 92.4 us -> 88.4 us (0.957)
  Pallas kernels: 91.6 us -> 87.6 us
    pallas_call x1, Pallas kernels: 82.2 us -> 78.3 us  [scores_and_gram(): pl.pallas_call(functools.partial(comm_kernel, scale, total_samples), out_...]
where the time goes in v4:
time: 88.4 us; the launch traced here: 88.3 us
  Pallas kernels  87.6 us (99%)
    pallas_call x1, Pallas kernels, scores_and_gram(): pl.pallas_call(functools.partial(comm_kernel, scale, total_samples), out_...  78.3 us
    pallas_call x1, Pallas kernels, factor_and_basis(): pl.pallas_call(functools.partial(factor_kernel, 8), out_shape=[jax.ShapeD...  9.37 us

profile of v4, /device:TPU:1, one launch (start us, length us, event | category | flops | bytes accessed | tf_op | source)
XLA Modules:
  0.0 88.3 jit_solution(1411917866883669401)
XLA Ops:
  0.6 78.3 %scores_and_gram.1 = (f32[768,256]{1,0:T(8,128)S(1)}, f32[256,256]{1,0:T(8,128)S(1)}) custom-call(bf16[768,2048]{1,0:T(8,128)(2,1)} %g_hbm.1, bf16[768,256]{1,0:T(8,128)(2,1)} %b_hbm.1), custom_call_target="tpu_custom_call" | custom-call | flops 1610612736 | bytes 3145728 | tf_op jit(solution)/shard_map/scores_and_gram/pallas_call | solution.py:261
  78.9 9.4 %factor_and_basis.1 = (f32[768,256]{1,0:T(8,128)}, f32[256,256]{1,0:T(8,128)}) custom-call(f32[256,256]{1,0:T(8,128)S(1)} %get-tuple-element.4.gram, f32[768,256]{1,0:T(8,128)S(1)} %get-tuple-element.5.scores_hbm), custom_call_target="tpu_custom_call" | custom-call | tf_op jit(solution)/shard_map/factor_and_basis/pallas_call | solution.py:378

commit v5 on v4

--- a/solution.py
+++ b/solution.py
@@ -200,20 +200,52 @@
     r = jnp.concatenate(r, axis=1)
     sall[rows(mine, chunk)] = r
     gp[...] = dot(r, r, ((0,), (0,)), precision=lax.Precision.HIGHEST) * (1.0 / total)
+
+    def each_core(core, body):
+        @pl.when(core == 0)
+        def _():
+            body(slice(None))
+
+        @pl.when(core == 1)
+        def _():
+            body(pl.ds(128, 128))
+
+    spot = (c * NX + x) * NY + y
     for i, (dy, dx, dc) in enumerate(plane):
         to = (lax.rem(c + dc, NC) * NX + lax.rem(x + dx, NX)) * NY + lax.rem(y + dy, NY)
-        start(gp.at[rows(to, 8)], gprecv.at[i], ps.at[2], pr.at[2], dev(0, dy, dx, dc))
+
+        def send_part(lanes, i=i, to=to, p=(dy, dx, dc)):
+            start(gp.at[rows(to, 8), lanes], gprecv.at[i, :, lanes], ps.at[2], pr.at[2], dev(0, *p))
+
+        each_core(lax.rem(c + dc, NC), send_part)
+
+    def sum_plane(lanes):
+        wait(gprecv.at[:, :, lanes], pr.at[2])
+        s = gp[rows(spot, 8), lanes]
+        for i in range(len(plane)):
+            s = s + gprecv[i, :, lanes]
+        gzall[z, :, lanes] = s
+        for dz in far:
+            own = gzall.at[z, :, lanes]
+            start(own, own, ps.at[6], pr.at[6], dev(dz, 0, 0, 0))
+
+    each_core(c, sum_plane)
     for dx in (2, 1, 3):
         own = sall.at[rows(mine, chunk)]
         start(own, own, ps.at[4], pr.at[4], dev(0, 0, dx, 0))
-    wait(gprecv, pr.at[2])
-    spot = (c * NX + x) * NY + y
-    s = gp[rows(spot, 8)]
-    for i in range(len(plane)):
-        s = s + gprecv[i]
-    gzall[z] = s
-    for dz in far:
-        start(gzall.at[z], gzall.at[z], ps.at[6], pr.at[6], dev(dz, 0, 0, 0))
+
+    def sum_z(lanes):
+        wait(gzall.at[pl.ds(0, NZ - 1), :, lanes], pr.at[6])
+        s = gzall[0, :, lanes]
+        for i in range(1, NZ):
+            s = s + gzall[i, :, lanes]
+        own = gram_ref.at[rows(spot, 8), lanes]
+        own[...] = s
+        for p in plane:
+            start(own, own, ps.at[8], pr.at[8], dev(0, *p))
+
+    each_core(c, sum_z)
+    gram_ref[128:, :128] = jnp.zeros((128, 128), F32)
     wait(sall.at[pl.ds(0, 3 * chunk)], pr.at[4])
     own = sall.at[rows(c, half)]
     start(own, own, ps.at[7], pr.at[7], dev(0, 0, 0, 1))
@@ -223,17 +255,17 @@
     own = sall.at[rows(other, half)]
     keep2 = pltpu.make_async_copy(own, scores_ref.at[rows(other, half)], out_sem.at[1])
     keep2.start()
-    wait(gzall.at[pl.ds(0, NZ - 1)], pr.at[6])
-    s = gzall[0]
-    for i in range(1, NZ):
-        s = s + gzall[i]
-    own = gram_ref.at[rows(spot, 8)]
-    own[...] = s
-    for p in plane:
-        start(own, own, ps.at[8], pr.at[8], dev(0, *p))
     keep.wait()
     keep2.wait()
-    wait(gram_ref.at[pl.ds(0, 248)], pr.at[8])
+
+    @pl.when(c == 0)
+    def _():
+        wait(spart.at[0, pl.ds(0, 368)], pr.at[8])
+
+    @pl.when(c == 1)
+    def _():
+        wait(spart.at[0, pl.ds(0, 376)], pr.at[8])
+
     for q in range(NQ):
         wait(ysend.at[q], ys.at[q])
         wait(zrecv.at[q], zs.at[q])
@@ -242,11 +274,22 @@
     for h in range(2):
         wait(crecv.at[h], cs.at[h])
         wait(xrecv.at[h], xs.at[h])
-    wait(gprecv, ps.at[2])
     wait(sall.at[pl.ds(0, 3 * chunk)], ps.at[4])
-    wait(gzall.at[pl.ds(0, NZ - 1)], ps.at[6])
     wait(sall.at[pl.ds(0, half)], ps.at[7])
-    wait(gram_ref.at[pl.ds(0, 248)], ps.at[8])
+
+    def sent(lanes):
+        wait(gzall.at[pl.ds(0, NZ - 1), :, lanes], ps.at[6])
+        wait(gprecv.at[:, :, lanes], ps.at[8])
+
+    each_core(c, sent)
+
+    @pl.when(c == 0)
+    def _():
+        wait(spart.at[0, pl.ds(0, 368)], ps.at[2])
+
+    @pl.when(c == 1)
+    def _():
+        wait(spart.at[0, pl.ds(0, 376)], ps.at[2])
 
 
 def scores_and_gram(genotypes, basis_in):

time: 88.4 us -> 86.1 us (0.974)
  Pallas kernels: 87.6 us -> 85.1 us
    pallas_call x1, Pallas kernels: 78.3 us -> 75.8 us  [scores_and_gram(): pl.pallas_call(functools.partial(comm_kernel, scale, total_samples), out_...]
where the time goes in v5:
time: 86.1 us; the launch traced here: 85.9 us
  Pallas kernels  85.1 us (99%)
    pallas_call x1, Pallas kernels, scores_and_gram(): pl.pallas_call(functools.partial(comm_kernel, scale, total_samples), out_...  75.8 us
    pallas_call x1, Pallas kernels, factor_and_basis(): pl.pallas_call(functools.partial(factor_kernel, 8), out_shape=[jax.ShapeD...  9.37 us

profile of v5, /device:TPU:1, one launch (start us, length us, event | category | flops | bytes accessed | tf_op | source)
XLA Modules:
  0.0 85.9 jit_solution(9783908615115251472)
XLA Ops:
  0.6 75.8 %scores_and_gram.1 = (f32[768,256]{1,0:T(8,128)S(1)}, f32[256,256]{1,0:T(8,128)S(1)}) custom-call(bf16[768,2048]{1,0:T(8,128)(2,1)} %g_hbm.1, bf16[768,256]{1,0:T(8,128)(2,1)} %b_hbm.1), custom_call_target="tpu_custom_call" | custom-call | flops 1610612736 | bytes 3145728 | tf_op jit(solution)/shard_map/scores_and_gram/pallas_call | solution.py:304
  76.4 9.4 %factor_and_basis.1 = (f32[768,256]{1,0:T(8,128)}, f32[256,256]{1,0:T(8,128)}) custom-call(f32[256,256]{1,0:T(8,128)S(1)} %get-tuple-element.4.gram, f32[768,256]{1,0:T(8,128)S(1)} %get-tuple-element.5.scores_hbm), custom_call_target="tpu_custom_call" | custom-call | tf_op jit(solution)/shard_map/factor_and_basis/pallas_call | solution.py:421

commit v6 on v5

--- a/solution.py
+++ b/solution.py
@@ -50,14 +50,14 @@
 
 def comm_kernel(
     scale, total, g_hbm, b_hbm, scores_ref, gram_ref,
-    bbuf, gbuf, tf, ysend, yrecv, sf, zsend, zrecv, lall,
+    bbuf, gbuf, tf, psend, precv, ysend, yrecv, sf, zsend, zrecv, lall,
     spart, crecv, xsend, xrecv, sall, gp, gprecv, gzall,
-    load_sem, out_sem, known, ys, yr, zs, zr, ls, lr, us, ur, cs, cr, xs, xr, ps, pr,
+    load_sem, out_sem, known, ks, kr, ys, yr, zs, zr, ls, lr, us, ur, ws, wr, cs, cr, xs, xr, ps, pr,
 ):
     samp, var = lax.axis_index("samples"), lax.axis_index("variants")
     z, y = lax.div(samp, NY), lax.rem(samp, NY)
     x, c = lax.div(var, NC), lax.rem(var, NC)
-    odd = lax.rem(z, 2)
+    pair = lax.div(z, 2)
 
     def dev(dz, dy, dx, dc):
         return (
@@ -85,7 +85,6 @@
     far = sorted(range(1, NZ), key=lambda d: -hops(d, NZ))
     near = [(dz, 0, 0, 0) for dz in (2, 14, 1, 15)] + [(0, dy, 0, 0) for dy in (2, 1, 3)]
     near += [(0, 0, dx, 0) for dx in (2, 1, 3)] + [(0, 0, 0, 1)]
-    units = [(q, h) for q in range(NQ) for h in range(2)]
 
     load_b = pltpu.make_async_copy(b_hbm, bbuf, load_sem.at[NQ])
     load_b.start()
@@ -106,74 +105,115 @@
         for i in range(NY):
             tf[q, i] = t[:, i * 128:(i + 1) * 128]
 
-    def send_y(q):
+    units = [(q, h) for q in range(NQ) for h in range(2)]
+
+    def parity(h):
+        return lax.rem(z + h, 2)
+
+    def partner(h):
+        return dev(1 + 14 * parity(h), 0, 0, 0)
+
+    def keep(h):
+        return rows(2 * h + parity(h), 64)
+
+    def send_pair(q):
         for h in range(2):
-            for dy in (2, 1, 3):
-                to = lax.rem(y + dy, NY)
-                ysend[q, h, dy - 1] = encode(tf[q, to, h * 128:(h + 1) * 128])
-                start(ysend.at[q, h, dy - 1], yrecv.at[q, h, dy - 1], ys.at[q], yr.at[q, h], dev(0, dy, 0, 0))
+            for i in range(NY):
+                psend[q, h, i] = encode(tf[q, i, rows(2 * h + 1 - parity(h), 64)])
+            start(psend.at[q, h], precv.at[q, h], ks.at[q], kr.at[q, h], partner(h))
+
+    def send_y(q, h):
+        wait(precv.at[q, h], kr.at[q, h])
+        for dy in (2, 1, 3, 0):
+            to = lax.rem(y + dy, NY)
+            s = tf[q, to, keep(h)] + decode(precv[q, h, to])
+            if dy == 0:
+                sf[q, h] = s
+                continue
+            ysend[q, h, dy - 1] = encode(s)
+            start(ysend.at[q, h, dy - 1], yrecv.at[q, h, dy - 1], ys.at[q], yr.at[q, h], dev(0, dy, 0, 0))
+
+    def send_z(q, h):
+        wait(yrecv.at[q, h], yr.at[q, h])
+        s = sf[q, h]
+        for i in range(NY - 1):
+            s = s + decode(yrecv[q, h, i])
+        sf[q, h] = s
+        zsend[q, h] = encode(s)
+        shift = lax.rem(pair + q, 2)
+        for i in (2, 1, 3, 0):
+            def send_tile(i=i):
+                d = 2 * i + shift
+                to = lax.div(lax.rem(pair + d, 8), 2)
+                start(
+                    zsend.at[q, h, rows(to, 16)], zrecv.at[q, h, rows(d - 1, 16)],
+                    zs.at[q], zr.at[q, h], dev(2 * d, 0, 0, 0),
+                )
+            if i:
+                send_tile()
+            else:
+                pl.when(shift == 1)(send_tile)
+
+    def finish_tile(q, h):
+        @pl.when(lax.rem(pair + q, 2) == 0)
+        def _():
+            wait(zrecv.at[q, h], zr.at[q, h])
+            s = sf[q, h, rows(lax.div(pair, 2), 16)]
+            for i in range(7):
+                s = s + decode(zrecv[q, h, i * 16:(i + 1) * 16])
+            tile = rows(8 * h + 4 * parity(h) + lax.div(pair, 2), 16)
+            lall[q, y, tile] = s.astype(BF16)
+            for d in (4, 3, 5, 2, 6, 1, 7):
+                mine = lall.at[q, y, tile]
+                start(mine, mine, ls.at[q], lr.at[q, h], dev(2 * d, 0, 0, 0))
+
+    def gather_y(q, h):
+        @pl.when(lax.rem(pair + q, 2) == 0)
+        def _():
+            wait(lall.at[q, y, pl.ds(0, 48)], lr.at[q, h])
+
+        @pl.when(lax.rem(pair + q, 2) == 1)
+        def _():
+            wait(lall.at[q, y, pl.ds(0, 64)], lr.at[q, h])
+
+        for dy in (2, 1, 3):
+            mine = lall.at[q, y, keep(h)]
+            start(mine, mine, us.at[q], ur.at[q, h], dev(0, dy, 0, 0))
+
+    def gather_pair(q, h):
+        wait(yrecv.at[q, h], ur.at[q, h])
+        mine = lall.at[q, :, keep(h)]
+        start(mine, mine, ws.at[q], wr.at[q, h], partner(h))
 
     load_b.wait()
     term(0)
     pl.semaphore_wait(barrier, len(near))
     for dz in (2, 14):
         signal(known.at[0], dev(dz, 0, 0, 0))
-    send_y(0)
+    send_pair(0)
     term(1)
-    send_y(1)
+    send_pair(1)
     pl.semaphore_wait(known.at[0], 2)
     for dz in (4, 12):
         signal(known.at[1], dev(dz, 0, 0, 0))
     for q in range(2, NQ):
         term(q)
-        send_y(q)
-    pl.semaphore_wait(known.at[1], 2)
-    for q, h in units:
-        wait(yrecv.at[q, h], yr.at[q, h])
-        s = tf[q, y, h * 128:(h + 1) * 128]
-        for i in range(NY - 1):
-            s = s + decode(yrecv[q, h, i])
-        sf[q, h] = s
-        zsend[q, h] = encode(s)
-        par = lax.rem(z + h, 2)
-        for i in (4, 3, 5, 2, 6, 1, 7, 0):
-            def send_tile(i=i):
-                d = 2 * i + par
-                to = lax.rem(z + d, NZ)
-                start(
-                    zsend.at[q, h, rows(lax.div(to, 2), 16)], zrecv.at[q, rows(d - 1, 16)],
-                    zs.at[q], zr.at[q], dev(d, 0, 0, 0),
-                )
-            if i:
-                send_tile()
-            else:
-                pl.when(par == 1)(send_tile)
-    tile = odd * 8 + lax.div(z, 2)
-    for q in range(NQ):
-        wait(zrecv.at[q], zr.at[q])
-        s = sf[q, odd, rows(lax.div(z, 2), 16)]
-        for i in range(NZ - 1):
-            s = s + decode(zrecv[q, i * 16:(i + 1) * 16])
-        lall[q, y, rows(tile, 16)] = s.astype(BF16)
-        for dz in far:
-            mine = lall.at[q, y, rows(tile, 16)]
-            start(mine, mine, ls.at[q], lr.at[q, odd], dev(dz, 0, 0, 0))
-    for q, h in units:
-        @pl.when(odd == h)
-        def _():
-            wait(lall.at[q, y, pl.ds(0, 112)], lr.at[q, h])
-
-        @pl.when(odd != h)
-        def _():
-            wait(lall.at[q, y, pl.ds(0, 128)], lr.at[q, h])
-
-        for dy in (2, 1, 3):
-            mine = lall.at[q, y, pl.ds(h * 128, 128)]
-            start(mine, mine, us.at[q], ur.at[q, h], dev(0, dy, 0, 0))
+        send_pair(q)
+    late = 5
+    for u in range(len(units) + late):
+        if u < len(units):
+            send_y(*units[u])
+        if u == late:
+            pl.semaphore_wait(known.at[1], 2)
+        if u >= late:
+            send_z(*units[u - late])
+    for u in units:
+        finish_tile(*u)
     half, chunk = spart.shape[1] // NC, spart.shape[1] // (NC * NX)
     other = lax.rem(c + 1, NC)
-    for q, h in units:
-        wait(yrecv.at[q, h], ur.at[q, h])
+
+    def score_term(q, h):
+        wait(precv.at[q, h], wr.at[q, h])
         part = jnp.concatenate([lall[q, i, h * 128:(h + 1) * 128] for i in range(NY)], axis=1)
         t = dot(gbuf[q], part, ((1,), (1,)))
         if q == 0:
@@ -182,6 +222,14 @@
             spart[h] += t
         if q == NQ - 1:
             start(spart.at[h, rows(other, half)], crecv.at[h], cs.at[h], cr.at[h], dev(0, 0, 0, 1))
+
+    for u in range(len(units) + 9):
+        if u < len(units):
+            gather_y(*units[u])
+        if 5 <= u < len(units) + 5:
+            gather_pair(*units[u - 5])
+        if u >= 9:
+            score_term(*units[u - 9])
     for h in range(2):
         wait(crecv.at[h], cr.at[h])
         crecv[h] = crecv[h] + spart[h, rows(c, half)]
@@ -249,14 +297,14 @@
     wait(sall.at[pl.ds(0, 3 * chunk)], pr.at[4])
     own = sall.at[rows(c, half)]
     start(own, own, ps.at[7], pr.at[7], dev(0, 0, 0, 1))
-    keep = pltpu.make_async_copy(own, scores_ref.at[rows(c, half)], out_sem.at[0])
-    keep.start()
+    out1 = pltpu.make_async_copy(own, scores_ref.at[rows(c, half)], out_sem.at[0])
+    out1.start()
     wait(sall.at[pl.ds(0, half)], pr.at[7])
     own = sall.at[rows(other, half)]
-    keep2 = pltpu.make_async_copy(own, scores_ref.at[rows(other, half)], out_sem.at[1])
-    keep2.start()
-    keep.wait()
-    keep2.wait()
+    out2 = pltpu.make_async_copy(own, scores_ref.at[rows(other, half)], out_sem.at[1])
+    out2.start()
+    out1.wait()
+    out2.wait()
 
     @pl.when(c == 0)
     def _():
@@ -267,10 +315,20 @@
         wait(spart.at[0, pl.ds(0, 376)], pr.at[8])
 
     for q in range(NQ):
+        wait(psend.at[q], ks.at[q])
         wait(ysend.at[q], ys.at[q])
-        wait(zrecv.at[q], zs.at[q])
-        wait(zrecv.at[q], ls.at[q])
-        wait(lall.at[q, pl.ds(0, 3)], us.at[q])
+        wait(ysend.at[q], us.at[q])
+        wait(psend.at[q], ws.at[q])
+
+        @pl.when(lax.rem(pair + q, 2) == 0)
+        def _():
+            wait(lall.at[q, 0, pl.ds(0, 96)], zs.at[q])
+            wait(zrecv.at[q], ls.at[q])
+
+        @pl.when(lax.rem(pair + q, 2) == 1)
+        def _():
+            wait(lall.at[q, 0, pl.ds(0, 128)], zs.at[q])
+
     for h in range(2):
         wait(crecv.at[h], cs.at[h])
         wait(xrecv.at[h], xs.at[h])
@@ -310,11 +368,13 @@
             pltpu.VMEM((n, k), BF16),
             pltpu.VMEM((NQ, n, part), BF16),
             pltpu.VMEM((NQ, NY, k, 128), F32),
-            pltpu.VMEM((NQ, 2, NY - 1, k // 2, 128), BF16),
-            pltpu.VMEM((NQ, 2, NY - 1, k // 2, 128), BF16),
-            pltpu.VMEM((NQ, 2, k // 2, 128), F32),
-            pltpu.VMEM((NQ, 2, k // 2, 128), BF16),
-            pltpu.VMEM((NQ, (NZ - 1) * 16, 128), BF16),
+            pltpu.VMEM((NQ, 2, NY, k // 4, 128), BF16),
+            pltpu.VMEM((NQ, 2, NY, k // 4, 128), BF16),
+            pltpu.VMEM((NQ, 2, NY - 1, k // 4, 128), BF16),
+            pltpu.VMEM((NQ, 2, NY - 1, k // 4, 128), BF16),
+            pltpu.VMEM((NQ, 2, k // 4, 128), F32),
+            pltpu.VMEM((NQ, 2, k // 4, 128), BF16),
+            pltpu.VMEM((NQ, 2, 7 * 16, 128), BF16),
             pltpu.VMEM((NQ, NY, k, 128), BF16),
             pltpu.VMEM((2, n, k // 2), F32),
             pltpu.VMEM((2, n // NC, k // 2), F32),
@@ -325,8 +385,8 @@
             pltpu.VMEM((NX * NY * NC - 1, 8, k), F32),
             pltpu.VMEM((NZ, 8, k), F32),
             dma((NQ + 1,)), dma((2,)), pltpu.SemaphoreType.REGULAR((2,)),
-            dma((NQ,)), dma((NQ, 2)), dma((NQ,)), dma((NQ,)),
-            dma((NQ,)), dma((NQ, 2)), dma((NQ,)), dma((NQ, 2)),
+            dma((NQ,)), dma((NQ, 2)), dma((NQ,)), dma((NQ, 2)), dma((NQ,)), dma((NQ, 2)),
+            dma((NQ,)), dma((NQ, 2)), dma((NQ,)), dma((NQ, 2)), dma((NQ,)), dma((NQ, 2)),
             dma((2,)), dma((2,)), dma((2,)), dma((2,)),
             dma((9,)), dma((9,)),
         ],

time: 86.1 us -> 85.5 us (level)
  no operation moved by 1% of the time
where the time goes in v6:
time: 85.5 us; the launch traced here: 85.4 us
  Pallas kernels  84.6 us (99%)
    pallas_call x1, Pallas kernels, scores_and_gram(): pl.pallas_call(functools.partial(comm_kernel, scale, total_samples), out_...  75.2 us
    pallas_call x1, Pallas kernels, factor_and_basis(): pl.pallas_call(functools.partial(factor_kernel, 8), out_shape=[jax.ShapeD...  9.37 us

profile of v6, /device:TPU:1, one launch (start us, length us, event | category | flops | bytes accessed | tf_op | source)
XLA Modules:
  0.0 85.4 jit_solution(3089446898245821398)
XLA Ops:
  0.6 75.2 %scores_and_gram.1 = (f32[768,256]{1,0:T(8,128)S(1)}, f32[256,256]{1,0:T(8,128)S(1)}) custom-call(bf16[768,2048]{1,0:T(8,128)(2,1)} %g_hbm.1, bf16[768,256]{1,0:T(8,128)(2,1)} %b_hbm.1), custom_call_target="tpu_custom_call" | custom-call | flops 1610612736 | bytes 3145728 | tf_op jit(solution)/shard_map/scores_and_gram/pallas_call | solution.py:362
  75.8 9.4 %factor_and_basis.1 = (f32[768,256]{1,0:T(8,128)}, f32[256,256]{1,0:T(8,128)}) custom-call(f32[256,256]{1,0:T(8,128)S(1)} %get-tuple-element.4.gram, f32[768,256]{1,0:T(8,128)S(1)} %get-tuple-element.5.scores_hbm), custom_call_target="tpu_custom_call" | custom-call | tf_op jit(solution)/shard_map/factor_and_basis/pallas_call | solution.py:481

commit v7 on v6

--- a/solution.py
+++ b/solution.py
@@ -110,8 +110,8 @@
     def parity(h):
         return lax.rem(z + h, 2)
 
-    def partner(h):
-        return dev(1 + 14 * parity(h), 0, 0, 0)
+    def partner(h, dy=0):
+        return dev(1 + 14 * parity(h), dy, 0, 0)
 
     def keep(h):
         return rows(2 * h + parity(h), 64)
@@ -121,6 +121,17 @@
             for i in range(NY):
                 psend[q, h, i] = encode(tf[q, i, rows(2 * h + 1 - parity(h), 64)])
             start(psend.at[q, h], precv.at[q, h], ks.at[q], kr.at[q, h], partner(h))
+
+    def send_direct(q):
+        for h in range(2):
+            for dy in (2, 1, 3, 0):
+                to = lax.rem(y + dy, NY)
+                psend[q, h, dy] = encode(tf[q, to, rows(2 * h + 1 - parity(h), 64)])
+                start(psend.at[q, h, dy], precv.at[q, h, dy], ks.at[q], kr.at[q, h], partner(h, dy))
+            for dy in (2, 1, 3):
+                to = lax.rem(y + dy, NY)
+                ysend[q, h, dy - 1] = encode(tf[q, to, keep(h)])
+                start(ysend.at[q, h, dy - 1], yrecv.at[q, h, dy - 1], ys.at[q], yr.at[q, h], dev(0, dy, 0, 0))
 
     def send_y(q, h):
         wait(precv.at[q, h], kr.at[q, h])
@@ -135,7 +146,13 @@
 
     def send_z(q, h):
         wait(yrecv.at[q, h], yr.at[q, h])
-        s = sf[q, h]
+        if q == NQ - 1:
+            wait(precv.at[q, h], kr.at[q, h])
+            s = tf[q, y, keep(h)]
+            for i in range(NY):
+                s = s + decode(precv[q, h, i])
+        else:
+            s = sf[q, h]
         for i in range(NY - 1):
             s = s + decode(yrecv[q, h, i])
         sf[q, h] = s
@@ -176,8 +193,11 @@
         def _():
             wait(lall.at[q, y, pl.ds(0, 64)], lr.at[q, h])
 
+        mine = lall.at[q, y, keep(h)]
+        if q == NQ - 1:
+            for dy in (2, 1, 3, 0):
+                start(mine, mine, ws.at[q], wr.at[q, h], partner(h, dy))
         for dy in (2, 1, 3):
-            mine = lall.at[q, y, keep(h)]
             start(mine, mine, us.at[q], ur.at[q, h], dev(0, dy, 0, 0))
 
     def gather_pair(q, h):
@@ -190,46 +210,59 @@
     pl.semaphore_wait(barrier, len(near))
     for dz in (2, 14):
         signal(known.at[0], dev(dz, 0, 0, 0))
+    for dz in (1, 15):
+        signal(known.at[2], dev(dz, 0, 0, 0))
     send_pair(0)
     term(1)
     send_pair(1)
     pl.semaphore_wait(known.at[0], 2)
     for dz in (4, 12):
         signal(known.at[1], dev(dz, 0, 0, 0))
-    for q in range(2, NQ):
-        term(q)
-        send_pair(q)
-    late = 5
-    for u in range(len(units) + late):
-        if u < len(units):
-            send_y(*units[u])
-        if u == late:
-            pl.semaphore_wait(known.at[1], 2)
-        if u >= late:
-            send_z(*units[u - late])
+    term(2)
+    send_pair(2)
+    term(3)
+    pl.semaphore_wait(known.at[2], 2)
+    send_direct(3)
+    for u in range(5):
+        send_y(*units[u])
+    pl.semaphore_wait(known.at[1], 2)
+    send_z(*units[0])
+    send_y(*units[5])
+    for u in range(1, 8):
+        send_z(*units[u])
     for u in units:
         finish_tile(*u)
     half, chunk = spart.shape[1] // NC, spart.shape[1] // (NC * NX)
     other = lax.rem(c + 1, NC)
 
-    def score_term(q, h):
-        wait(precv.at[q, h], wr.at[q, h])
-        part = jnp.concatenate([lall[q, i, h * 128:(h + 1) * 128] for i in range(NY)], axis=1)
+    def score_term(q, halves):
+        for h in halves:
+            if q == NQ - 1:
+                wait(yrecv.at[q, h], ur.at[q, h])
+            wait(precv.at[q, h], wr.at[q, h])
+        lo, hi = 128 * halves[0], 128 * (halves[-1] + 1)
+        part = jnp.concatenate([lall[q, i, lo:hi] for i in range(NY)], axis=1)
         t = dot(gbuf[q], part, ((1,), (1,)))
-        if q == 0:
-            spart[h] = t
-        else:
-            spart[h] += t
-        if q == NQ - 1:
-            start(spart.at[h, rows(other, half)], crecv.at[h], cs.at[h], cr.at[h], dev(0, 0, 0, 1))
-
-    for u in range(len(units) + 9):
-        if u < len(units):
-            gather_y(*units[u])
-        if 5 <= u < len(units) + 5:
+        for i, h in enumerate(halves):
+            if q == 0:
+                spart[h] = t[:, i * 128:(i + 1) * 128]
+            else:
+                spart[h] += t[:, i * 128:(i + 1) * 128]
+            if q == NQ - 1:
+                start(spart.at[h, rows(other, half)], crecv.at[h], cs.at[h], cr.at[h], dev(0, 0, 0, 1))
+
+    for u in range(len(units)):
+        gather_y(*units[u])
+        if u >= 5:
             gather_pair(*units[u - 5])
-        if u >= 9:
-            score_term(*units[u - 9])
+    for u in (3, 4, 5):
+        gather_pair(*units[u])
+    score_term(0, (0, 1))
+    score_term(1, (0, 1))
+    score_term(2, (0,))
+    score_term(3, (0,))
+    score_term(2, (1,))
+    score_term(3, (1,))
     for h in range(2):
         wait(crecv.at[h], cr.at[h])
         crecv[h] = crecv[h] + spart[h, rows(c, half)]
@@ -259,13 +292,16 @@
             body(pl.ds(128, 128))
 
     spot = (c * NX + x) * NY + y
-    for i, (dy, dx, dc) in enumerate(plane):
-        to = (lax.rem(c + dc, NC) * NX + lax.rem(x + dx, NX)) * NY + lax.rem(y + dy, NY)
-
-        def send_part(lanes, i=i, to=to, p=(dy, dx, dc)):
-            start(gp.at[rows(to, 8), lanes], gprecv.at[i, :, lanes], ps.at[2], pr.at[2], dev(0, *p))
-
-        each_core(lax.rem(c + dc, NC), send_part)
+    for core in range(NC):
+        @pl.when(c == core)
+        def _():
+            for i, (dy, dx, dc) in enumerate(plane):
+                lanes = pl.ds(128, 128) if (core + dc) % NC else slice(None)
+                to = ((core + dc) % NC * NX + lax.rem(x + dx, NX)) * NY + lax.rem(y + dy, NY)
+                start(
+                    gp.at[rows(to, 8), lanes], gprecv.at[i, :, lanes],
+                    ps.at[2], pr.at[2], dev(0, dy, dx, dc),
+                )
 
     def sum_plane(lanes):
         wait(gprecv.at[:, :, lanes], pr.at[2])
@@ -384,7 +420,7 @@
             pltpu.VMEM((k, k), F32),
             pltpu.VMEM((NX * NY * NC - 1, 8, k), F32),
             pltpu.VMEM((NZ, 8, k), F32),
-            dma((NQ + 1,)), dma((2,)), pltpu.SemaphoreType.REGULAR((2,)),
+            dma((NQ + 1,)), dma((2,)), pltpu.SemaphoreType.REGULAR((3,)),
             dma((NQ,)), dma((NQ, 2)), dma((NQ,)), dma((NQ, 2)), dma((NQ,)), dma((NQ, 2)),
             dma((NQ,)), dma((NQ, 2)), dma((NQ,)), dma((NQ, 2)), dma((NQ,)), dma((NQ, 2)),
             dma((2,)), dma((2,)), dma((2,)), dma((2,)),

time: 85.5 us -> 85.8 us (level)
  no operation moved by 1% of the time
where the time goes in v7:
time: 85.8 us; the launch traced here: 85.7 us
  Pallas kernels  84.9 us (99%)
    pallas_call x1, Pallas kernels, scores_and_gram(): pl.pallas_call(functools.partial(comm_kernel, scale, total_samples), out_...  75.5 us
    pallas_call x1, Pallas kernels, factor_and_basis(): pl.pallas_call(functools.partial(factor_kernel, 8), out_shape=[jax.ShapeD...  9.37 us

profile of v7, /device:TPU:1, one launch (start us, length us, event | category | flops | bytes accessed | tf_op | source)
XLA Modules:
  0.0 85.7 jit_solution(12763018165923431187)
XLA Ops:
  0.6 75.5 %scores_and_gram.1 = (f32[768,256]{1,0:T(8,128)S(1)}, f32[256,256]{1,0:T(8,128)S(1)}) custom-call(bf16[768,2048]{1,0:T(8,128)(2,1)} %g_hbm.1, bf16[768,256]{1,0:T(8,128)(2,1)} %b_hbm.1), custom_call_target="tpu_custom_call" | custom-call | flops 1610612736 | bytes 3145728 | tf_op jit(solution)/shard_map/scores_and_gram/pallas_call | solution.py:398
  76.2 9.4 %factor_and_basis.1 = (f32[768,256]{1,0:T(8,128)}, f32[256,256]{1,0:T(8,128)}) custom-call(f32[256,256]{1,0:T(8,128)S(1)} %get-tuple-element.4.gram, f32[768,256]{1,0:T(8,128)S(1)} %get-tuple-element.5.scores_hbm), custom_call_target="tpu_custom_call" | custom-call | tf_op jit(solution)/shard_map/factor_and_basis/pallas_call | solution.py:517

commit v8 on v7

--- a/solution.py
+++ b/solution.py
@@ -10,6 +10,7 @@
 MESH = pl.DeviceIdType.MESH
 NZ, NY, NX, NC = 16, 4, 4, 2
 NQ = 4
+LATE = 5
 F32, BF16 = jnp.float32, jnp.bfloat16
 SHIFT = 4096.0
 LOG_SHIFT = 8.317766166719343
@@ -122,17 +123,6 @@
                 psend[q, h, i] = encode(tf[q, i, rows(2 * h + 1 - parity(h), 64)])
             start(psend.at[q, h], precv.at[q, h], ks.at[q], kr.at[q, h], partner(h))
 
-    def send_direct(q):
-        for h in range(2):
-            for dy in (2, 1, 3, 0):
-                to = lax.rem(y + dy, NY)
-                psend[q, h, dy] = encode(tf[q, to, rows(2 * h + 1 - parity(h), 64)])
-                start(psend.at[q, h, dy], precv.at[q, h, dy], ks.at[q], kr.at[q, h], partner(h, dy))
-            for dy in (2, 1, 3):
-                to = lax.rem(y + dy, NY)
-                ysend[q, h, dy - 1] = encode(tf[q, to, keep(h)])
-                start(ysend.at[q, h, dy - 1], yrecv.at[q, h, dy - 1], ys.at[q], yr.at[q, h], dev(0, dy, 0, 0))
-
     def send_y(q, h):
         wait(precv.at[q, h], kr.at[q, h])
         for dy in (2, 1, 3, 0):
@@ -146,13 +136,7 @@
 
     def send_z(q, h):
         wait(yrecv.at[q, h], yr.at[q, h])
-        if q == NQ - 1:
-            wait(precv.at[q, h], kr.at[q, h])
-            s = tf[q, y, keep(h)]
-            for i in range(NY):
-                s = s + decode(precv[q, h, i])
-        else:
-            s = sf[q, h]
+        s = sf[q, h]
         for i in range(NY - 1):
             s = s + decode(yrecv[q, h, i])
         sf[q, h] = s
@@ -210,26 +194,22 @@
     pl.semaphore_wait(barrier, len(near))
     for dz in (2, 14):
         signal(known.at[0], dev(dz, 0, 0, 0))
-    for dz in (1, 15):
-        signal(known.at[2], dev(dz, 0, 0, 0))
     send_pair(0)
     term(1)
     send_pair(1)
     pl.semaphore_wait(known.at[0], 2)
     for dz in (4, 12):
         signal(known.at[1], dev(dz, 0, 0, 0))
-    term(2)
-    send_pair(2)
-    term(3)
-    pl.semaphore_wait(known.at[2], 2)
-    send_direct(3)
-    for u in range(5):
-        send_y(*units[u])
-    pl.semaphore_wait(known.at[1], 2)
-    send_z(*units[0])
-    send_y(*units[5])
-    for u in range(1, 8):
-        send_z(*units[u])
+    for q in range(2, NQ):
+        term(q)
+        send_pair(q)
+    for u in range(len(units) + LATE):
+        if u < len(units):
+            send_y(*units[u])
+        if u == LATE:
+            pl.semaphore_wait(known.at[1], 2)
+        if u >= LATE:
+            send_z(*units[u - LATE])
     for u in units:
         finish_tile(*u)
     half, chunk = spart.shape[1] // NC, spart.shape[1] // (NC * NX)
@@ -251,12 +231,13 @@
             if q == NQ - 1:
                 start(spart.at[h, rows(other, half)], crecv.at[h], cs.at[h], cr.at[h], dev(0, 0, 0, 1))
 
-    for u in range(len(units)):
-        gather_y(*units[u])
-        if u >= 5:
-            gather_pair(*units[u - 5])
-    for u in (3, 4, 5):
-        gather_pair(*units[u])
+    queue = [u for u in units if u[0] != NQ - 1]
+    for i, u in enumerate(units):
+        gather_y(*u)
+        if i >= LATE and queue:
+            gather_pair(*queue.pop(0))
+    for u in queue:
+        gather_pair(*u)
     score_term(0, (0, 1))
     score_term(1, (0, 1))
     score_term(2, (0,))
@@ -328,6 +309,24 @@
         for p in plane:
             start(own, own, ps.at[8], pr.at[8], dev(0, *p))
 
+    for q in range(NQ):
+        wait(psend.at[q], ks.at[q])
+        wait(ysend.at[q], ys.at[q])
+        wait(ysend.at[q], us.at[q])
+        wait(psend.at[q], ws.at[q])
+
+        @pl.when(lax.rem(pair + q, 2) == 0)
+        def _():
+            wait(lall.at[q, 0, pl.ds(0, 96)], zs.at[q])
+            wait(zrecv.at[q], ls.at[q])
+
+        @pl.when(lax.rem(pair + q, 2) == 1)
+        def _():
+            wait(lall.at[q, 0, pl.ds(0, 128)], zs.at[q])
+
+    for h in range(2):
+        wait(crecv.at[h], cs.at[h])
+        wait(xrecv.at[h], xs.at[h])
     each_core(c, sum_z)
     gram_ref[128:, :128] = jnp.zeros((128, 128), F32)
     wait(sall.at[pl.ds(0, 3 * chunk)], pr.at[4])
@@ -350,24 +349,6 @@
     def _():
         wait(spart.at[0, pl.ds(0, 376)], pr.at[8])
 
-    for q in range(NQ):
-        wait(psend.at[q], ks.at[q])
-        wait(ysend.at[q], ys.at[q])
-        wait(ysend.at[q], us.at[q])
-        wait(psend.at[q], ws.at[q])
-
-        @pl.when(lax.rem(pair + q, 2) == 0)
-        def _():
-            wait(lall.at[q, 0, pl.ds(0, 96)], zs.at[q])
-            wait(zrecv.at[q], ls.at[q])
-
-        @pl.when(lax.rem(pair + q, 2) == 1)
-        def _():
-            wait(lall.at[q, 0, pl.ds(0, 128)], zs.at[q])
-
-    for h in range(2):
-        wait(crecv.at[h], cs.at[h])
-        wait(xrecv.at[h], xs.at[h])
     wait(sall.at[pl.ds(0, 3 * chunk)], ps.at[4])
     wait(sall.at[pl.ds(0, half)], ps.at[7])
 
@@ -420,7 +401,7 @@
             pltpu.VMEM((k, k), F32),
             pltpu.VMEM((NX * NY * NC - 1, 8, k), F32),
             pltpu.VMEM((NZ, 8, k), F32),
-            dma((NQ + 1,)), dma((2,)), pltpu.SemaphoreType.REGULAR((3,)),
+            dma((NQ + 1,)), dma((2,)), pltpu.SemaphoreType.REGULAR((2,)),
             dma((NQ,)), dma((NQ, 2)), dma((NQ,)), dma((NQ, 2)), dma((NQ,)), dma((NQ, 2)),
             dma((NQ,)), dma((NQ, 2)), dma((NQ,)), dma((NQ, 2)), dma((NQ,)), dma((NQ, 2)),
             dma((2,)), dma((2,)), dma((2,)), dma((2,)),
@@ -485,7 +466,7 @@
     return dot(ah, bh, dims) + (dot(ah, bl, dims) + dot(al, bh, dims))
 
 
-def factor_kernel(panel, gram, scores_hbm, basis_hbm, factor, scores, basis, sems):
+def factor_kernel(panel, gram, scores_hbm, basis_hbm, factor_hbm, scores, basis, factor, sems):
     n = gram.shape[0]
     h = n // 2
     load = pltpu.make_async_copy(scores_hbm, scores, sems.at[0])
@@ -496,19 +477,23 @@
     a22 = gram[h:, h:] - dot(u12, u12, ((0,), (0,)), precision=lax.Precision.HIGHEST)
     first = dot3(scores[:, :h], v1, ((1,), (1,)))
     rest = scores[:, h:] - dot3(first, u12, ((1,), (0,)))
-    u22, v2 = eliminate(a22, panel)
-    basis[0] = first
-    basis[1] = dot3(rest, v2, ((1,), (1,)))
-    out1 = pltpu.make_async_copy(basis.at[0], basis_hbm.at[:, pl.ds(0, h)], sems.at[1])
-    out1.start()
-    out2 = pltpu.make_async_copy(basis.at[1], basis_hbm.at[:, pl.ds(h, h)], sems.at[2])
-    out2.start()
     factor[:h, :h] = u11
     factor[:h, h:] = u12
     factor[h:, :h] = jnp.zeros((h, h), F32)
+    basis[0] = first
+    u22, v2 = eliminate(a22, panel)
     factor[h:, h:] = u22
-    out1.wait()
-    out2.wait()
+    outs = [
+        pltpu.make_async_copy(factor, factor_hbm, sems.at[3]),
+        pltpu.make_async_copy(basis.at[0], basis_hbm.at[:, pl.ds(0, h)], sems.at[1]),
+        pltpu.make_async_copy(basis.at[1], basis_hbm.at[:, pl.ds(h, h)], sems.at[2]),
+    ]
+    outs[0].start()
+    outs[1].start()
+    basis[1] = dot3(rest, v2, ((1,), (1,)))
+    outs[2].start()
+    for out in outs:
+        out.wait()
 
 
 def factor_and_basis(gram, scores):
@@ -518,11 +503,12 @@
         functools.partial(factor_kernel, 8),
         out_shape=[jax.ShapeDtypeStruct(scores.shape, F32), jax.ShapeDtypeStruct(gram.shape, F32)],
         in_specs=[vmem, hbm],
-        out_specs=[hbm, vmem],
+        out_specs=[hbm, hbm],
         scratch_shapes=[
             pltpu.VMEM((n, k), F32),
             pltpu.VMEM((2, n, k // 2), F32),
-            pltpu.SemaphoreType.DMA((3,)),
+            pltpu.VMEM((k, k), F32),
+            pltpu.SemaphoreType.DMA((4,)),
         ],
         compiler_params=pltpu.CompilerParams(vmem_limit_bytes=40 << 20),
         name="factor_and_basis",

time: 85.8 us -> 83.6 us (0.974)
  Pallas kernels: 84.9 us -> 82.7 us
    pallas_call x1, Pallas kernels: 75.5 us -> 74 us  [scores_and_gram(): pl.pallas_call(functools.partial(comm_kernel, scale, total_samples), out_...]
where the time goes in v8:
time: 83.6 us; the launch traced here: 83.5 us
  Pallas kernels  82.7 us (99%)
    pallas_call x1, Pallas kernels, scores_and_gram(): pl.pallas_call(functools.partial(comm_kernel, scale, total_samples), out_...  74 us
    pallas_call x1, Pallas kernels, factor_and_basis(): pl.pallas_call(functools.partial(factor_kernel, 8), out_shape=[jax.ShapeD...  8.66 us

profile of v8, /device:TPU:1, one launch (start us, length us, event | category | flops | bytes accessed | tf_op | source)
XLA Modules:
  0.0 83.5 jit_solution(5917180127438821090)
XLA Ops:
  0.6 74.0 %scores_and_gram.1 = (f32[768,256]{1,0:T(8,128)S(1)}, f32[256,256]{1,0:T(8,128)S(1)}) custom-call(bf16[768,2048]{1,0:T(8,128)(2,1)} %g_hbm.1, bf16[768,256]{1,0:T(8,128)(2,1)} %b_hbm.1), custom_call_target="tpu_custom_call" | custom-call | flops 1610612736 | bytes 3145728 | tf_op jit(solution)/shard_map/scores_and_gram/pallas_call | solution.py:379
  74.7 8.7 %factor_and_basis.1 = (f32[768,256]{1,0:T(8,128)}, f32[256,256]{1,0:T(8,128)}) custom-call(f32[256,256]{1,0:T(8,128)S(1)} %get-tuple-element.4.gram, f32[768,256]{1,0:T(8,128)S(1)} %get-tuple-element.5.scores_hbm), custom_call_target="tpu_custom_call" | custom-call | tf_op jit(solution)/shard_map/factor_and_basis/pallas_call | solution.py:502

commit v9 on v8

--- a/solution.py
+++ b/solution.py
@@ -119,15 +119,16 @@
 
     def send_pair(q):
         for h in range(2):
-            for i in range(NY):
-                psend[q, h, i] = encode(tf[q, i, rows(2 * h + 1 - parity(h), 64)])
-            start(psend.at[q, h], precv.at[q, h], ks.at[q], kr.at[q, h], partner(h))
+            for dy in (2, 1, 3, 0):
+                to = lax.rem(y + dy, NY)
+                psend[q, h, dy] = encode(tf[q, to, rows(2 * h + 1 - parity(h), 64)])
+                start(psend.at[q, h, dy], precv.at[q, h, dy], ks.at[q], kr.at[q, h, dy], partner(h))
 
     def send_y(q, h):
-        wait(precv.at[q, h], kr.at[q, h])
         for dy in (2, 1, 3, 0):
             to = lax.rem(y + dy, NY)
-            s = tf[q, to, keep(h)] + decode(precv[q, h, to])
+            wait(precv.at[q, h, dy], kr.at[q, h, dy])
+            s = tf[q, to, keep(h)] + decode(precv[q, h, dy])
             if dy == 0:
                 sf[q, h] = s
                 continue
@@ -195,14 +196,13 @@
     for dz in (2, 14):
         signal(known.at[0], dev(dz, 0, 0, 0))
     send_pair(0)
-    term(1)
-    send_pair(1)
-    pl.semaphore_wait(known.at[0], 2)
-    for dz in (4, 12):
-        signal(known.at[1], dev(dz, 0, 0, 0))
-    for q in range(2, NQ):
+    for q in range(1, NQ):
         term(q)
         send_pair(q)
+        if q == 2:
+            pl.semaphore_wait(known.at[0], 2)
+            for dz in (4, 12):
+                signal(known.at[1], dev(dz, 0, 0, 0))
     for u in range(len(units) + LATE):
         if u < len(units):
             send_y(*units[u])
@@ -222,14 +222,19 @@
             wait(precv.at[q, h], wr.at[q, h])
         lo, hi = 128 * halves[0], 128 * (halves[-1] + 1)
         part = jnp.concatenate([lall[q, i, lo:hi] for i in range(NY)], axis=1)
+        if q == NQ - 1:
+            h, = halves
+            for core in (other, c):
+                spart[h, rows(core, half)] += dot(gbuf[q, rows(core, half)], part, ((1,), (1,)))
+                if core is other:
+                    start(spart.at[h, rows(other, half)], crecv.at[h], cs.at[h], cr.at[h], dev(0, 0, 0, 1))
+            return
         t = dot(gbuf[q], part, ((1,), (1,)))
         for i, h in enumerate(halves):
             if q == 0:
                 spart[h] = t[:, i * 128:(i + 1) * 128]
             else:
                 spart[h] += t[:, i * 128:(i + 1) * 128]
-            if q == NQ - 1:
-                start(spart.at[h, rows(other, half)], crecv.at[h], cs.at[h], cr.at[h], dev(0, 0, 0, 1))
 
     queue = [u for u in units if u[0] != NQ - 1]
     for i, u in enumerate(units):
@@ -259,9 +264,11 @@
         for i in range(NX - 1):
             s = s + decode_wide(xrecv[h, i])
         r.append(s * scale)
-    r = jnp.concatenate(r, axis=1)
-    sall[rows(mine, chunk)] = r
-    gp[...] = dot(r, r, ((0,), (0,)), precision=lax.Precision.HIGHEST) * (1.0 / total)
+        sall[rows(mine, chunk), h * 128:(h + 1) * 128] = r[h]
+        for i in range(h + 1):
+            gp[i * 128:(i + 1) * 128, h * 128:(h + 1) * 128] = (
+                dot(r[i], r[h], ((0,), (0,)), precision=lax.Precision.HIGHEST) * (1.0 / total)
+            )
 
     def each_core(core, body):
         @pl.when(core == 0)
@@ -402,7 +409,7 @@
             pltpu.VMEM((NX * NY * NC - 1, 8, k), F32),
             pltpu.VMEM((NZ, 8, k), F32),
             dma((NQ + 1,)), dma((2,)), pltpu.SemaphoreType.REGULAR((2,)),
-            dma((NQ,)), dma((NQ, 2)), dma((NQ,)), dma((NQ, 2)), dma((NQ,)), dma((NQ, 2)),
+            dma((NQ,)), dma((NQ, 2, NY)), dma((NQ,)), dma((NQ, 2)), dma((NQ,)), dma((NQ, 2)),
             dma((NQ,)), dma((NQ, 2)), dma((NQ,)), dma((NQ, 2)), dma((NQ,)), dma((NQ, 2)),
             dma((2,)), dma((2,)), dma((2,)), dma((2,)),
             dma((9,)), dma((9,)),

time: 83.6 us -> 82.3 us (0.984)
  Pallas kernels: 82.7 us -> 81.4 us
    pallas_call x1, Pallas kernels: 74 us -> 72.8 us  [scores_and_gram(): pl.pallas_call(functools.partial(comm_kernel, scale, total_samples), out_...]
where the time goes in v9:
time: 82.3 us; the launch traced here: 82.2 us
  Pallas kernels  81.4 us (99%)
    pallas_call x1, Pallas kernels, scores_and_gram(): pl.pallas_call(functools.partial(comm_kernel, scale, total_samples), out_...  72.8 us
    pallas_call x1, Pallas kernels, factor_and_basis(): pl.pallas_call(functools.partial(factor_kernel, 8), out_shape=[jax.ShapeD...  8.66 us

profile of v9, /device:TPU:1, one launch (start us, length us, event | category | flops | bytes accessed | tf_op | source)
XLA Modules:
  0.0 82.2 jit_solution(16295368081373983975)
XLA Ops:
  0.6 72.8 %scores_and_gram.1 = (f32[768,256]{1,0:T(8,128)S(1)}, f32[256,256]{1,0:T(8,128)S(1)}) custom-call(bf16[768,2048]{1,0:T(8,128)(2,1)} %g_hbm.1, bf16[768,256]{1,0:T(8,128)(2,1)} %b_hbm.1), custom_call_target="tpu_custom_call" | custom-call | flops 1610612736 | bytes 3145728 | tf_op jit(solution)/shard_map/scores_and_gram/pallas_call | solution.py:386
  73.4 8.7 %factor_and_basis.1 = (f32[768,256]{1,0:T(8,128)}, f32[256,256]{1,0:T(8,128)}) custom-call(f32[256,256]{1,0:T(8,128)S(1)} %get-tuple-element.4.gram, f32[768,256]{1,0:T(8,128)S(1)} %get-tuple-element.5.scores_hbm), custom_call_target="tpu_custom_call" | custom-call | tf_op jit(solution)/shard_map/factor_and_basis/pallas_call | solution.py:509

commit v10 on v9

--- a/solution.py
+++ b/solution.py
@@ -334,13 +334,13 @@
     for h in range(2):
         wait(crecv.at[h], cs.at[h])
         wait(xrecv.at[h], xs.at[h])
-    each_core(c, sum_z)
-    gram_ref[128:, :128] = jnp.zeros((128, 128), F32)
     wait(sall.at[pl.ds(0, 3 * chunk)], pr.at[4])
     own = sall.at[rows(c, half)]
     start(own, own, ps.at[7], pr.at[7], dev(0, 0, 0, 1))
     out1 = pltpu.make_async_copy(own, scores_ref.at[rows(c, half)], out_sem.at[0])
     out1.start()
+    each_core(c, sum_z)
+    gram_ref[128:, :128] = jnp.zeros((128, 128), F32)
     wait(sall.at[pl.ds(0, half)], pr.at[7])
     own = sall.at[rows(other, half)]
     out2 = pltpu.make_async_copy(own, scores_ref.at[rows(other, half)], out_sem.at[1])

time: 82.3 us -> 82.3 us (level)
  no operation moved by 1% of the time
where the time goes in v10:
time: 82.3 us; the launch traced here: 82.2 us
  Pallas kernels  81.4 us (99%)
    pallas_call x1, Pallas kernels, scores_and_gram(): pl.pallas_call(functools.partial(comm_kernel, scale, total_samples), out_...  72.8 us
    pallas_call x1, Pallas kernels, factor_and_basis(): pl.pallas_call(functools.partial(factor_kernel, 8), out_shape=[jax.ShapeD...  8.66 us

profile of v10, /device:TPU:1, one launch (start us, length us, event | category | flops | bytes accessed | tf_op | source)
XLA Modules:
  0.0 82.2 jit_solution(9895299212898372304)
XLA Ops:
  0.6 72.8 %scores_and_gram.1 = (f32[768,256]{1,0:T(8,128)S(1)}, f32[256,256]{1,0:T(8,128)S(1)}) custom-call(bf16[768,2048]{1,0:T(8,128)(2,1)} %g_hbm.1, bf16[768,256]{1,0:T(8,128)(2,1)} %b_hbm.1), custom_call_target="tpu_custom_call" | custom-call | flops 1610612736 | bytes 3145728 | tf_op jit(solution)/shard_map/scores_and_gram/pallas_call | solution.py:386
  73.4 8.7 %factor_and_basis.1 = (f32[768,256]{1,0:T(8,128)}, f32[256,256]{1,0:T(8,128)}) custom-call(f32[256,256]{1,0:T(8,128)S(1)} %get-tuple-element.4.gram, f32[768,256]{1,0:T(8,128)S(1)} %get-tuple-element.5.scores_hbm), custom_call_target="tpu_custom_call" | custom-call | tf_op jit(solution)/shard_map/factor_and_basis/pallas_call | solution.py:509
